TPU v7x, 512 devices: a whole 4x4x16 slice. The times are simulated.
512 devices in a mesh: dp: 64 (over y, z), tensor: 8 (over x, core).
Axes of the slice: x: 4, y: 4, z: 16, core: 2. Of those that a mesh axis runs over, the one named last changes fastest.
Arguments:
- grad_values: bfloat16 [64, 128, 4, 6144], P('dp', None, None, 'tensor'), may hold values from -24 to 24
- grad_scales: float32 [64, 128], P('dp'), may hold values from 0.25 to 4
- owner_ids: int32 [128, 1], replicated, may hold values from 0 to 63; in each aligned block of 128 rows (0 to 127, 128 to 255, ...) at most 4 rows name the same one
- step_count: int32 [1], replicated, may hold values from 1 to 3
- master: bfloat16 [64, 4, 4, 6144], P('dp', None, None, 'tensor'), may hold values from -4 to 4
- moment1: bfloat16 [64, 4, 4, 6144], P('dp', None, None, 'tensor'), may hold values from -0.59765625 to 0.59765625
- moment2: bfloat16 [64, 4, 4, 6144], P('dp', None, None, 'tensor'), may hold values from 0.0049743652 to 0.19921875
Outputs:
- new_master: bfloat16 [64, 4, 4, 6144], P('dp', None, None, 'tensor')
- new_moment1: bfloat16 [64, 4, 4, 6144], P('dp', None, None, 'tensor')
- new_moment2: bfloat16 [64, 4, 4, 6144], P('dp', None, None, 'tensor')
- quantized: bfloat16 [128, 4, 6144], P(None, None, 'tensor')
- weight_scales: float32 [128], replicated
Inputs may be any that keep to these rules, and one draw needn't show every extreme that they name: `owner_ids`: each of the 64 owners holds 1 to 4 tensors, and some owner holds exactly 4.
All inputs are finite; a program needn't handle non-finite values. Where the computation divides by a largest or mean magnitude, that divisor is 1e-20 or more.
Results may differ from a plain program's by a relative error of at most 0.015.
Values may be sent and summed in bfloat16 or wider, within the bound.
A program may use at most 64 MiB of HBM per device.

v0:
```python
import jax
import jax.numpy as jnp
from jax import lax
from jax.sharding import PartitionSpec as P

BETA_ONE = 0.9
BETA_TWO = 0.95
RATE = 0.1
DECAY = 0.1
ADAM_EPS = 1e-08
PEAK_EPS = 1e-06
CLIP_RMS = 0.5


def slot_ranks(owner_list):
    count = owner_list.shape[0]
    same = (owner_list[:, None] == owner_list[None, :]).astype(jnp.int32)
    earlier = (jnp.arange(count)[None, :] < jnp.arange(count)[:, None]).astype(jnp.int32)
    return jnp.sum(same * earlier, axis=1)


def adam_update(summed, factor, step_count, master, moment1, moment2):
    step_value = step_count[0].astype(jnp.float32)
    clipped = summed * factor
    first = BETA_ONE * moment1.astype(jnp.float32) + (1.0 - BETA_ONE) * clipped
    second = BETA_TWO * moment2.astype(jnp.float32) + (1.0 - BETA_TWO) * clipped * clipped
    first_hat = first / (1.0 - jnp.power(jnp.float32(BETA_ONE), step_value))
    second_hat = second / (1.0 - jnp.power(jnp.float32(BETA_TWO), step_value))
    weight = master.astype(jnp.float32)
    updated = weight - RATE * (first_hat / (jnp.sqrt(second_hat) + ADAM_EPS) + DECAY * weight)
    return (updated.astype(jnp.bfloat16), first.astype(jnp.bfloat16), second.astype(jnp.bfloat16))


def local(grad_values, grad_scales, owner_ids, step_count, master, moment1, moment2):
    owner_list = owner_ids[:, 0]
    tensors = owner_list.shape[0]
    slots = master.shape[1]
    rows = master.shape[2]
    columns = master.shape[3]
    replicas = lax.axis_size("dp")
    my_index = lax.axis_index("dp")
    slot_of = slot_ranks(owner_list)
    positions = owner_list * slots + slot_of
    slot_iota = jnp.arange(slots, dtype=jnp.int32)
    my_slots = (owner_list[None, :] == my_index) & (slot_of[None, :] == slot_iota[:, None])
    live_slots = jnp.any(my_slots, axis=1)
    local_terms = grad_values[0].astype(jnp.float32) * grad_scales[0][:, None, None]
    buffer = (
        jnp.zeros((replicas * slots, rows, columns), jnp.float32).at[positions].set(local_terms)
    )
    summed = lax.psum_scatter(buffer, "dp", scatter_dimension=0, tiled=True)
    squares = lax.psum(jnp.sum(summed * summed), ("dp", "tensor"))
    element_count = float(tensors * rows * columns * lax.axis_size("tensor"))
    factor = jnp.minimum(
        1.0, CLIP_RMS * jnp.sqrt(jnp.float32(element_count)) / jnp.sqrt(squares + 1e-06)
    )
    old_w = master[0]
    old_m = moment1[0]
    old_v = moment2[0]
    new_w, new_m, new_v = adam_update(summed, factor, step_count, old_w, old_m, old_v)
    keep = live_slots[:, None, None]
    new_w = jnp.where(keep, new_w, old_w)
    new_m = jnp.where(keep, new_m, old_m)
    new_v = jnp.where(keep, new_v, old_v)
    owned = new_w.astype(jnp.float32)
    slot_peak = jnp.max(jnp.abs(owned), axis=(1, 2))
    slot_scales = lax.pmax(slot_peak, "tensor") + PEAK_EPS
    scaled_slots = (owned / slot_scales[:, None, None]).astype(jnp.bfloat16)
    every_scaled, every_scale = (
        lax.all_gather(scaled_slots, "dp", axis=0, tiled=True),
        lax.all_gather(slot_scales.astype(jnp.bfloat16), "dp", axis=0, tiled=True).astype(
            slot_scales.dtype
        ),
    )
    quantized = every_scaled[positions]
    weight_scales = every_scale[positions]
    return (new_w[None], new_m[None], new_v[None], quantized, weight_scales)


def solution(mesh):
    return jax.shard_map(
        local,
        mesh=mesh,
        in_specs=(
            P("dp", None, None, "tensor"),
            P("dp", None),
            P(),
            P(),
            P("dp", None, None, "tensor"),
            P("dp", None, None, "tensor"),
            P("dp", None, None, "tensor"),
        ),
        out_specs=(
            P("dp", None, None, "tensor"),
            P("dp", None, None, "tensor"),
            P("dp", None, None, "tensor"),
            P(None, None, "tensor"),
            P(),
        ),
        check_vma=False,
    )
```

profile of v0, /device:TPU:32, one launch (start us, length us, event | category | flops | bytes accessed | tf_op | source)
XLA Modules:
  0.0 584.8 jit_solution(546450022670621982)
XLA Ops:
  7.2 0.0 all-reduce.4.cloned.1.call-start
  7.2 0.9 select_reduce_fusion
  8.1 0.7 fusion.11
  8.8 2.8 convert_multiply_fusion
  11.6 0.4 broadcast_in_dim.36
  12.0 11.7 %scatter_fusion = f32[256,4,768]{2,1,0:T(4,128)S(1)} fusion(f32[256,4,768]{2,1,0:T(4,128)S(1)} %broadcast_in_dim.36, s32[128]{0:T(128)S(1)} %fusion.11, f32[128,4,768]{2,1,0:T(4,128)} %convert_multiply_fusion), kind=kCustom, calls=%fused_computation.2 | custom fusion | bytes 4719104 | tf_op jit(solution)/shard_map/scatter | solution.py:49
  23.7 0.0 copy-start
  23.7 0.0 copy-start.5
  23.7 0.0 copy-start.6
  23.7 0.0 copy-start.1
  23.7 0.0 copy-start.2
  23.8 0.0 copy-start.4
  23.8 1.6 copy-done
  25.4 0.0 all-reduce.4.cloned.1.call-update
  25.4 0.0 all-gather.2.cloned.1.call-start
  26.2 0.0 copy-done.5
  26.2 0.6 fusion.14
  27.5 0.0 copy-done.6
  27.5 0.1 fusion.10
  27.6 285.6 %all-reduce.4.cloned.1.call-done = f32[256,4,768]{2,1,0:T(4,128)} async-done(((f32[256,4,768]{2,1,0:T(4,128)}), f32[256,4,768]{2,1,0:T(4,128)}) %all-reduce.4.cloned.1.call-update) | async-done | bytes 3145744
  313.2 1.4 multiply_reduce_fusion
  314.7 100.9 %psum.7 = f32[]{:T(128)} all-reduce(f32[]{:T(128)} %multiply_reduce_fusion), channel_id=1, replica_groups=mesh['dp'=64,'tensor'=8] {'dp','tensor'}, use_global_device_ids=true, to_apply=%region_5.0 | all-reduce | flops 1 | bytes 8 | tf_op jit(solution)/shard_map/psum | solution.py:52
  416.2 0.0 copy-done.1
  416.2 1.0 fusion.3
  417.3 13.4 %pmax.7 = f32[4]{0:T(128)S(1)} all-reduce(f32[4]{0:T(128)S(1)} %get-tuple-element.5), channel_id=1, replica_groups=mesh['dp'=64,'tensor'=8] {'tensor'}, use_global_device_ids=true, to_apply=%region_7.8 | all-reduce | flops 4 | bytes 32 | tf_op jit(solution)/shard_map/pmax | solution.py:67
  430.7 0.7 fusion.4
  431.4 0.0 all-gather.2.cloned.1.call-update
  432.0 0.2 dynamic-update-slice
  432.3 138.9 %all-reduce = bf16[256]{0:T(256)(128)(2,1)S(1)} all-reduce(bf16[256]{0:T(256)(128)(2,1)S(1)} %dynamic-update-slice), channel_id=1, replica_groups=mesh['dp'=64,'tensor'=8] {'dp'}, use_global_device_ids=true, to_apply=%add | all-reduce | flops 256 | bytes 1024
  571.2 1.8 gather_fusion.1
  573.0 1.5 fusion.7
  574.5 3.5 gather_fusion
  (10 shorter events, 0.0 us)
Async XLA Ops:
  7.2 306.1 %all-reduce.4.cloned.1.call-start = ((), (), s32[]{:S(2)}) async-start(), calls=%async_computation.1 | async-start | bytes 6291456
  23.7 1.7 copy-start
  23.7 2.5 copy-start.5
  23.7 3.7 copy-start.6
  23.7 392.5 %copy-start.1 = (bf16[1,4,4,768]{3,2,1,0:T(4,128)(2,1)S(1)}, bf16[1,4,4,768]{3,2,1,0:T(4,128)(2,1)}, u32[]{:S(2)}) copy-start(bf16[1,4,4,768]{3,2,1,0:T(4,128)(2,1)} %param.13) | copy-start | bytes 73732
  23.7 392.5 %copy-start.2 = (bf16[1,4,4,768]{3,2,1,0:T(4,128)(2,1)S(1)}, bf16[1,4,4,768]{3,2,1,0:T(4,128)(2,1)}, u32[]{:S(2)}) copy-start(bf16[1,4,4,768]{3,2,1,0:T(4,128)(2,1)} %param.12) | copy-start | bytes 73732
  23.8 392.5 %copy-start.4 = (bf16[1,4,4,768]{3,2,1,0:T(4,128)(2,1)S(1)}, bf16[1,4,4,768]{3,2,1,0:T(4,128)(2,1)}, u32[]{:S(2)}) copy-start(bf16[1,4,4,768]{3,2,1,0:T(4,128)(2,1)} %param.11) | copy-start | bytes 73732
  25.4 549.1 %all-gather.2.cloned.1.call-start = ((), (), s32[]{:S(2)}) async-start(), calls=%async_computation | async-start | bytes 1597440 | tf_op jit(solution)/shard_map/all_gather | solution.py:70
  417.3 160.7 %copy-start.3 = (bf16[4,4,768]{2,1,0:T(4,128)(2,1)}, bf16[4,4,768]{2,1,0:T(4,128)(2,1)S(1)}, u32[]{:S(2)}) copy-start(bf16[4,4,768]{2,1,0:T(4,128)(2,1)S(1)} %get-tuple-element.6) | copy-start | bytes 73732
Sparse Core Ops, SparseCore 0:
  25.5 287.6 all-reduce.3
  431.5 131.4 all-gather.1
where the time goes:
time: 585 us
  waiting for transfers between devices  286 us (49%)
  blocking collectives  253 us (43%)
  local copies, waits for them, and re-layouts  19.9 us (3%)
  between operations  16.9 us (3%)
  other arithmetic  9.14 us (2%)
    unnamed x3, waiting for transfers between devices  286 us
    unnamed x1, blocking collectives  139 us
    psum x1, blocking collectives, local(): squares = lax.psum(jnp.sum(summed * summed), ('dp', 'tensor'))  101 us
    pmax x1, blocking collectives, local(): slot_scales = lax.pmax(slot_peak, 'tensor') + PEAK_EPS  13.4 us
    scatter x1, local copies, waits for them, and re-layouts, local(): jnp.zeros((replicas * slots, rows, columns), jnp.float32).at[positions]  11.7 us
  transfers between devices with their start and end apart: 2, of which 1 were waited for; matrix products, arithmetic and copies ran while one was open for 1% of the time, Pallas kernels for 0%

commit v1 on v0

v1 whole, which is shorter than its diff:
```python
import jax
import jax.numpy as jnp
from jax import lax
from jax.experimental import pallas as pl
from jax.experimental.pallas import tpu as pltpu
from jax.sharding import PartitionSpec as P

BETA_ONE = 0.9
BETA_TWO = 0.95
RATE = 0.1
DECAY = 0.1
ADAM_EPS = 1e-08
PEAK_EPS = 1e-06
CLIP_RMS = 0.5

NY, NZ, NX, NC = 4, 16, 4, 2
NT, SLOTS, R, COLS = 128, 4, 4, 768
CB = COLS // 128
BLKS = CB * R
E = BLKS * 128
YE = E // NY
PER = YE // NZ
YB = BLKS // NY
MESH = pl.DeviceIdType.MESH
BF, F32 = jnp.bfloat16, jnp.float32

_counts = dict(
    sy=3, sz=15, gy=48, gz=15, qz=15, qy=3, qt=7, dz=15, dy=3, az=15, ay=48, mz=15, my=3, mt=7
)
BASE, _total = {}, 0
for _name, _count in _counts.items():
    BASE[_name] = _total
    _total += _count


def offset_of(j):
    return 8 + (1 - 2 * (j % 2)) * ((j + 1) // 2)


def adam(g, step, master, first, second):
    m = BETA_ONE * first + (1.0 - BETA_ONE) * g
    v = BETA_TWO * second + (1.0 - BETA_TWO) * g * g
    one = 1.0 - jnp.exp(step * jnp.log(jnp.full_like(step, BETA_ONE)))
    two = 1.0 - jnp.exp(step * jnp.log(jnp.full_like(step, BETA_TWO)))
    m_hat = m / one
    v_hat = v / two
    w = master - RATE * (m_hat / (jnp.sqrt(v_hat) + ADAM_EPS) + DECAY * master)
    return w, m, v


def kernel(
    g_ref, gs_ref, own_ref, step_ref, w_ref, m_ref, v_ref,
    nw_ref, nm_ref, nv_ref, quant_ref, scale_ref,
    gv, fs, tv, sv, sf, ysf, ys, syr, st, szs, szr,
    yr, zs, zr, sbp, dsend, dr, dys, dyr, s2, nv,
    qsend, qzr, qys, qyr, qts, qtr,
    msend, mzr, mys, myr, mts, mtr,
    wown, agb, ov,
    lsem, ssem, rsem,
):
    dp, tp = lax.axis_index("dp"), lax.axis_index("tensor")
    y, z = dp // NZ, dp % NZ

    def at_z(zz):
        return (y * NZ + zz, tp)

    def at_y(yy):
        return (yy * NZ + z, tp)

    def at_t(tt):
        return (dp, tt)

    def send(kind, i, src, dst, dev):
        pltpu.make_async_remote_copy(
            src_ref=src, dst_ref=dst, send_sem=ssem.at[BASE[kind] + i],
            recv_sem=rsem.at[BASE[kind] + i], device_id=dev, device_id_type=MESH,
        ).start()

    def arrived(kind, i, ref):
        pltpu.make_async_copy(ref, ref, rsem.at[BASE[kind] + i]).wait()

    def sent(kind, count, ref):
        def body(i, carry):
            pltpu.make_async_copy(ref, ref, ssem.at[BASE[kind] + i]).wait()
            return carry
        lax.fori_loop(0, count, body, 0)

    state = (w_ref, m_ref, v_ref)

    def g_copy(cb):
        return pltpu.make_async_copy(g_ref.at[:, :, pl.ds(cb * 128, 128)], gv.at[cb], lsem.at[cb])

    def s_copy(a, cb):
        return pltpu.make_async_copy(
            state[a].at[:, :, pl.ds(cb * 128, 128)], sv.at[a, cb], lsem.at[CB + a * CB + cb]
        )

    for cb in range(CB):
        g_copy(cb).start()
    for a in range(3):
        for cb in range(CB):
            s_copy(a, cb).start()

    barrier = pltpu.get_barrier_semaphore()

    def greet(peers, device_of):
        def body(k, carry):
            pl.semaphore_signal(barrier, inc=1, device_id=device_of(k), device_id_type=MESH)
            return carry
        lax.fori_loop(1, peers, body, 0)

    greet(NZ, lambda k: at_z((z + k) % NZ))
    greet(NY, lambda k: at_y((y + k) % NY))
    greet(NX * NC, lambda k: at_t((tp + k) % (NX * NC)))

    scales = gs_ref[...]
    g2 = gv.reshape(CB, NT * R, 128)
    for cb in range(CB):
        g_copy(cb).wait()
        fs[...] = g2[cb].astype(F32)
        for r in range(R):
            block = fs[pl.ds(r, NT, stride=R), :]
            tv[pl.ds((cb * R + r) * 128, 128), :] = (block.T * scales).astype(BF)

    for a in range(3):
        for cb in range(CB):
            s_copy(a, cb).wait()
    sf[...] = sv.reshape(3 * CB * SLOTS * R, 128)[...].astype(F32)
    ysf[...] = jnp.zeros_like(ysf)
    for a in range(3):
        for r in range(R):
            rows = sf[pl.ds(a * CB * SLOTS * R + r, CB * SLOTS, stride=R), :]
            ysf[:, pl.ds(r * 16 + a * 4, 4), :] = rows.reshape(CB, SLOTS, 128)
    ys[...] = ysf[...].reshape(NY, YB * 16, 128).astype(BF)

    pl.semaphore_wait(barrier, (NZ - 1) + (NY - 1) + (NX * NC - 1))

    for k in range(1, NY):
        yy = (y + k) % NY
        send("sy", k - 1, ys.at[yy], syr.at[y], at_y(yy))

    def y_send(j, carry):
        zz = (z + offset_of(j)) % NZ
        for k in range(1, NY):
            yy = (y + k) % NY
            src = tv.at[pl.ds(pl.multiple_of((yy * NZ + zz) * PER, 16), PER)]
            send("gy", j * 3 + k - 1, src, yr.at[j, k - 1], at_y(yy))
        return carry

    lax.fori_loop(0, NZ, y_send, 0)

    def y_sum(j):
        zz = (z + offset_of(j)) % NZ
        total = tv[pl.ds(pl.multiple_of((y * NZ + zz) * PER, 16), PER), :].astype(F32)
        for k in range(3):
            arrived("gy", j * 3 + k, yr.at[j, k])
            total = total + yr[j, k].astype(F32)
        return total

    def z_send(j, carry):
        zz = (z + offset_of(j)) % NZ
        zs[j] = y_sum(j).astype(BF)
        send("gz", j, zs.at[j], zr.at[j], at_z(zz))
        return carry

    lax.fori_loop(0, NZ - 1, z_send, 0)
    mine = y_sum(NZ - 1)

    syr[y] = ys[y]
    for k in range(1, NY):
        arrived("sy", k - 1, syr.at[(y - k + NY) % NY])
    for b in range(YB):
        block = syr[:, pl.ds(b * 16, 16), :].reshape(NY * 16, 128).astype(F32)
        block = jnp.concatenate([block, jnp.zeros((128 - NY * 16, 128), F32)], axis=0)
        st[pl.ds(b * 128, 128), :] = block.T
    for zz in range(NZ):
        upper = st[pl.ds(zz * PER, 16), :] + pltpu.roll(st[pl.ds(zz * PER + 16, 16), :], 64, 1)
        szs[zz, pl.ds(0, 16), :] = upper.astype(BF)
        szs[zz, pl.ds(16, 16), :] = st[pl.ds(zz * PER + 32, 16), :].astype(BF)

    def sz_send(j, carry):
        zz = (z + offset_of(j)) % NZ
        send("sz", j, szs.at[zz], szr.at[z], at_z(zz))
        return carry

    lax.fori_loop(0, NZ - 1, sz_send, 0)
    szr[z] = szs[z]

    own = own_ref[...]
    spread = jnp.broadcast_to(own.astype(F32), (NT, NT))
    same = spread == spread.T
    before = lax.broadcasted_iota(jnp.int32, (NT, NT), 0) < lax.broadcasted_iota(jnp.int32, (NT, NT), 1)
    slot = jnp.sum(jnp.where(same & before, 1.0, 0.0), axis=0, keepdims=True).astype(jnp.int32)
    own_z, own_y = own & (NZ - 1), own >> 4
    count = jnp.sum(jnp.where(own == dp, 1.0, 0.0), axis=1, keepdims=True)
    place = own_z * 16 + own_y * 4 + slot
    hot = jnp.where(
        lax.broadcasted_iota(jnp.int32, (NZ * 16, NT), 0) == place, 1.0, 0.0
    ).astype(BF)

    def z_add(j, total):
        arrived("gz", j, zr.at[j])
        return total + zr[j].astype(F32)

    summed = lax.fori_loop(0, NZ - 1, z_add, mine)

    def z_stage(kind, value, sendbuf, buf):
        sendbuf[...] = value
        buf[z] = value

        def body(j, carry):
            send(kind, j, sendbuf, buf.at[z], at_z((z + offset_of(j)) % NZ))
            return carry

        lax.fori_loop(0, NZ - 1, body, 0)

    def z_wait(kind, buf):
        def body(j, carry):
            arrived(kind, j, buf.at[(z - offset_of(j) + NZ) % NZ])
            return carry

        lax.fori_loop(0, NZ - 1, body, 0)

    def y_stage(kind, value, sendbuf, buf):
        sendbuf[...] = value
        buf[y] = value
        for k in (2, 1, 3):
            send(kind, k - 1, sendbuf, buf.at[y], at_y((y + k) % NY))

    def y_wait(kind, buf):
        for k in range(1, NY):
            arrived(kind, k - 1, buf.at[(y - k + NY) % NY])

    def t_stage(kind, value, sendbuf, buf):
        sendbuf[...] = value
        buf[tp] = value
        for k in (4, 5, 3, 2, 6, 7, 1):
            send(kind, k - 1, sendbuf, buf.at[tp], at_t((tp + k) % (NX * NC)))

    def t_wait(kind, buf):
        for k in range(1, NX * NC):
            arrived(kind, k - 1, buf.at[(tp - k + NX * NC) % (NX * NC)])

    squares = jnp.sum((summed * summed).reshape(PER // 8, 8, 128), axis=0)
    z_stage("qz", squares, qsend, qzr)

    sum_bf = summed.astype(BF)
    sbp[...] = jnp.zeros_like(sbp)
    sbp[pl.ds(0, PER), :] = sum_bf
    dsend[...] = (
        lax.dot_general(hot, sbp[...], (((1,), (1,)), ((), ())), preferred_element_type=F32)
        .astype(BF)
        .reshape(NZ, 16, 128)
    )

    def d_send(j, carry):
        zz = (z + offset_of(j)) % NZ
        send("dz", j, dsend.at[zz], dr.at[z], at_z(zz))
        return carry

    lax.fori_loop(0, NZ - 1, d_send, 0)
    dr[z] = dsend[z]

    z_wait("sz", szr)
    low = lax.broadcasted_iota(jnp.int32, (16, 128), 1) < 64
    parts = [[], [], []]
    for pair in range(NZ // 2):
        even0, even1 = szr[2 * pair, pl.ds(0, 16), :].astype(F32), szr[2 * pair, pl.ds(16, 16), :].astype(F32)
        odd0, odd1 = szr[2 * pair + 1, pl.ds(0, 16), :].astype(F32), szr[2 * pair + 1, pl.ds(16, 16), :].astype(F32)
        parts[0].append(jnp.where(low, even0, pltpu.roll(odd0, 64, 1)))
        parts[1].append(jnp.where(low, pltpu.roll(even0, 64, 1), odd0))
        parts[2].append(jnp.where(low, even1, pltpu.roll(odd1, 64, 1)))
    packed = jnp.concatenate([jnp.concatenate(p, axis=1) for p in parts], axis=0).astype(BF)
    target = own_z * 64 + own_y * 16 + slot
    rows = lax.broadcasted_iota(jnp.int32, (NZ * 64, NT), 0)
    old = []
    for a in range(3):
        pick = jnp.where(rows == target + 4 * a, 1.0, 0.0).astype(BF)
        old.append(jnp.dot(packed, pick, preferred_element_type=F32))

    z_wait("qz", qzr)
    y_stage("qy", jnp.sum(qzr[...], axis=0), qys, qyr)
    y_wait("qy", qyr)
    t_stage("qt", jnp.sum(qyr[...], axis=0), qts, qtr)
    t_wait("qt", qtr)
    all_squares = jnp.sum(jnp.sum(qtr[...], axis=0), axis=(0, 1), keepdims=True)
    entries = float(NT * R * COLS * NX * NC)
    factor = jnp.minimum(
        1.0, CLIP_RMS * jnp.sqrt(jnp.full((1, 1), entries, F32)) / jnp.sqrt(all_squares + 1e-06)
    )
    step = jnp.full((1, 1), step_ref[0].astype(F32), F32)

    new_w, _, _ = adam(sum_bf.astype(F32) * factor, step, old[0], old[1], old[2])
    new_w = new_w.astype(BF)
    here = pl.multiple_of(dp * PER, 16)
    wown[...] = new_w
    agb[pl.ds(here, PER), :] = new_w

    def slice_at(ref, yy, zz):
        return ref.at[pl.ds(pl.multiple_of((yy * NZ + zz) * PER, 16), PER)]

    def a_send(j, carry):
        send("az", j, wown, slice_at(agb, y, z), at_z((z + offset_of(j)) % NZ))
        return carry

    lax.fori_loop(0, NZ - 1, a_send, 0)
    for k in range(1, NY):
        send("ay", (NZ - 1) * 3 + k - 1, wown, slice_at(agb, y, z), at_y((y + k) % NY))
    peak = jnp.max(jnp.abs(new_w.astype(F32)).reshape(PER // 8, 8, 128), axis=0)
    z_stage("mz", peak, msend, mzr)

    def a_forward(i, carry):
        j = NZ - 2 - i
        zz = (z - offset_of(j) + NZ) % NZ
        ref = slice_at(agb, y, zz)
        arrived("az", j, ref)
        for k in range(1, NY):
            send("ay", j * 3 + k - 1, ref, ref, at_y((y + k) % NY))
        return carry

    lax.fori_loop(0, NZ - 1, a_forward, 0)
    z_wait("mz", mzr)
    y_stage("my", jnp.max(mzr[...], axis=0), mys, myr)

    z_wait("dz", dr)
    lane = lax.broadcasted_iota(jnp.int32, (16, 128), 1)
    for b in range(YB):
        block = jnp.zeros((16, 128), F32)
        for zz in range(NZ):
            start = zz * PER - b * 128
            if -PER < start < 128:
                piece = dr[zz].astype(F32)
                if start % 128:
                    piece = pltpu.roll(piece, start % 128, 1)
                if start < 0:
                    piece = jnp.where(lane < start + PER, piece, 0.0)
                elif start + PER > 128:
                    piece = jnp.where(lane >= start, piece, 0.0)
                block = block + piece
        dys[:, pl.ds(b * 4, 4), :] = block.reshape(NY, SLOTS, 128)
    for k in range(1, NY):
        yy = (y + k) % NY
        send("dy", k - 1, dys.at[yy], dyr.at[y], at_y(yy))
    dyr[y] = dys[y]

    y_wait("my", myr)
    t_stage("mt", jnp.max(myr[...], axis=0), mts, mtr)

    y_wait("dy", dyr)
    flat = dyr.reshape(NY * YB * SLOTS, 128)
    for s in range(SLOTS):
        rows_s = flat[pl.ds(s, BLKS, stride=SLOTS), :]
        s2[:, pl.ds(s * R, R), :] = rows_s.reshape(CB, R, 128)
    sums = s2[...].reshape(CB * SLOTS * R, 128)
    size = CB * SLOTS * R
    olds = [sf[pl.ds(a * size, size), :] for a in range(3)]
    news = adam(sums * factor, step, *olds)
    slot_row = (lax.broadcasted_iota(jnp.int32, (size, 128), 0) // R) % SLOTS
    live = slot_row.astype(F32) < count
    nv2 = nv.reshape(3, size, 128)
    outs = (nw_ref, nm_ref, nv_ref)

    def o_copy(a, cb):
        return pltpu.make_async_copy(
            nv.at[a, cb], outs[a].at[:, :, pl.ds(cb * 128, 128)], lsem.at[CB + a * CB + cb]
        )

    for a in range(3):
        nv2[a] = jnp.where(live, news[a], olds[a]).astype(BF)
        for cb in range(CB):
            o_copy(a, cb).start()

    def a_wait(i, carry):
        j = NZ - 1 - i
        zz = (z - offset_of(j) + NZ) % NZ
        for k in range(1, NY):
            arrived("ay", j * 3 + k - 1, slice_at(agb, (y - k + NY) % NY, zz))
        return carry

    lax.fori_loop(0, NZ, a_wait, 0)
    t_wait("mt", mtr)
    peaks = jnp.max(jnp.max(mtr[...], axis=0), axis=0, keepdims=True) + PEAK_EPS
    scale_ref[...] = peaks
    inverse = 1.0 / peaks

    o2 = ov.reshape(CB, NT * R, 128)

    def q_copy(cb):
        return pltpu.make_async_copy(ov.at[cb], quant_ref.at[:, :, pl.ds(cb * 128, 128)], lsem.at[cb])

    for cb in range(CB):
        for r in range(R):
            block = agb[pl.ds((cb * R + r) * 128, 128), :].astype(F32) * inverse
            fs[pl.ds(r, NT, stride=R), :] = block.T
        o2[cb] = fs[...].astype(BF)
        q_copy(cb).start()

    sent("sy", 3, ys.at[0])
    sent("sz", 15, szs.at[0])
    sent("gy", 48, yr.at[0, 0])
    sent("gz", 15, zs.at[0])
    sent("qz", 15, qsend)
    sent("qy", 3, qys)
    sent("qt", 7, qts)
    sent("dz", 15, dsend.at[0])
    sent("dy", 3, dys.at[0])
    sent("az", 15, wown)
    sent("ay", 48, wown)
    sent("mz", 15, msend)
    sent("my", 3, mys)
    sent("mt", 7, mts)
    for a in range(3):
        for cb in range(CB):
            o_copy(a, cb).wait()
    for cb in range(CB):
        q_copy(cb).wait()


def local(grad_values, grad_scales, owner_ids, step_count, master, moment1, moment2):
    vmem = pl.BlockSpec(memory_space=pltpu.VMEM)
    smem = pl.BlockSpec(memory_space=pltpu.SMEM)
    anym = pl.BlockSpec(memory_space=pl.ANY)
    owned = jax.ShapeDtypeStruct((SLOTS, R, COLS), BF)
    V = pltpu.VMEM
    small = lambda n: V((n, 8, 128), F32)
    one = V((8, 128), F32)
    exchange = [one, small(NZ), one, small(NY), one, small(NX * NC)]
    out = pl.pallas_call(
        kernel,
        out_shape=(
            owned, owned, owned,
            jax.ShapeDtypeStruct((NT, R, COLS), BF),
            jax.ShapeDtypeStruct((1, NT), F32),
        ),
        in_specs=[anym, vmem, vmem, smem, anym, anym, anym],
        out_specs=(anym, anym, anym, anym, vmem),
        scratch_shapes=[
            V((CB, NT, R, 128), BF),
            V((NT * R, 128), F32),
            V((E, NT), BF),
            V((3, CB, SLOTS, R, 128), BF),
            V((3 * CB * SLOTS * R, 128), F32),
            V((CB, R * 16, 128), F32),
            V((NY, YB * 16, 128), BF),
            V((NY, YB * 16, 128), BF),
            V((YE, 128), F32),
            V((NZ, 32, 128), BF),
            V((NZ, 32, 128), BF),
            V((NZ, 3, PER, NT), BF),
            V((NZ, PER, NT), BF),
            V((NZ, PER, NT), BF),
            V((128, NT), BF),
            V((NZ, 16, 128), BF),
            V((NZ, 16, 128), BF),
            V((NY, YB * SLOTS, 128), F32),
            V((NY, YB * SLOTS, 128), F32),
            V((CB, SLOTS * R, 128), F32),
            V((3, CB, SLOTS, R, 128), BF),
        ]
        + exchange
        + exchange
        + [
            V((PER, NT), BF),
            V((E, NT), BF),
            V((CB, NT, R, 128), BF),
            pltpu.SemaphoreType.DMA((4 * CB,)),
            pltpu.SemaphoreType.DMA((_total,)),
            pltpu.SemaphoreType.DMA((_total,)),
        ],
        compiler_params=pltpu.CompilerParams(
            collective_id=0, has_side_effects=True, vmem_limit_bytes=40 << 20
        ),
    )(
        grad_values[0], grad_scales, owner_ids.reshape(1, NT), step_count,
        master[0], moment1[0], moment2[0],
    )
    return out[0][None], out[1][None], out[2][None], out[3], out[4].reshape(NT)


def solution(mesh):
    split = P("dp", None, None, "tensor")
    return jax.shard_map(
        local,
        mesh=mesh,
        in_specs=(split, P("dp", None), P(), P(), split, split, split),
        out_specs=(split, split, split, P(None, None, "tensor"), P()),
        check_vma=False,
    )
```

time: 585 us -> 91.4 us (0.16)
  the two profiles are of different devices: /device:TPU:32 before, /device:TPU:1 now
where the time goes in v1:
time: 91.4 us; the launch traced here: 91.1 us
  Pallas kernels  82.5 us (90%)
  local copies, waits for them, and re-layouts  7.21 us (8%)
  between operations  1.31 us (1%)
    pallas_call x1, Pallas kernels, local(): pl.pallas_call(kernel, out_shape=(owned, owned, owned, jax.ShapeDtypeStru...  82.5 us
    unnamed x17, local copies, waits for them, and re-layouts  7.21 us

profile of v1, /device:TPU:1, one launch (start us, length us, event | category | flops | bytes accessed | tf_op | source)
XLA Modules:
  0.0 91.1 jit_solution(3644068792406229313)
XLA Ops:
  1.3 0.0 copy-start.4
  1.3 0.0 copy-start.5
  1.3 0.6 copy-done.4
  1.9 0.0 copy-done.5
  2.0 0.0 copy-start
  2.0 1.1 %copy-done = bf16[1,128,4,768]{3,2,1,0:T(4,128)(2,1)S(1)} copy-done((bf16[1,128,4,768]{3,2,1,0:T(4,128)(2,1)S(1)}, bf16[1,128,4,768]{3,2,1,0:T(4,128)(2,1)}, u32[]{:S(2)}) %copy-start) | copy-done | bytes 786456
  3.1 0.0 copy-start.1
  3.1 0.7 copy-done.1
  3.8 0.0 copy-start.2
  3.8 0.7 copy-done.2
  4.6 0.0 copy-start.3
  4.6 0.7 copy-done.3
  5.3 82.5 %shard_map.110 = (bf16[4,4,768]{2,1,0:T(4,128)(2,1)S(1)}, bf16[4,4,768]{2,1,0:T(4,128)(2,1)S(1)}, bf16[4,4,768]{2,1,0:T(4,128)(2,1)S(1)}, bf16[128,4,768]{2,1,0:T(4,128)(2,1)S(1)}, f32[1,128]{1,0:T(1,128)S(1)}) custom-call(bf16[128,4,768]{2,1,0:T(4,128)(2,1)S(1)} %bitcast.9, f32[1,128]{1,0:T(1,128)S(1)} %copy-done.4, s32[1,128]{1,0:T(1,128)S(1)} %bitcast.16, ...), custom_call_target="tpu_custom_call" | custom-call | tf_op jit(solution)/shard_map/pallas_call | solution.py:428
  87.8 0.6 copy.18
  88.4 0.6 copy.19
  89.1 0.6 copy.20
  89.7 0.9 copy.21
  90.5 0.5 copy.22
Async XLA Ops:
  1.3 0.7 copy-start.4
  1.3 0.7 copy-start.5
  2.0 1.1 %copy-start = (bf16[1,128,4,768]{3,2,1,0:T(4,128)(2,1)S(1)}, bf16[1,128,4,768]{3,2,1,0:T(4,128)(2,1)}, u32[]{:S(2)}) copy-start(bf16[1,128,4,768]{3,2,1,0:T(4,128)(2,1)} %param.7) | copy-start | bytes 2359300
  3.1 0.7 copy-start.1
  3.8 0.7 copy-start.2
  4.6 0.7 copy-start.3

commit v2 on v1

v2 whole, which is shorter than its diff:
```python
import jax
import jax.numpy as jnp
from jax import lax
from jax.experimental import pallas as pl
from jax.experimental.pallas import tpu as pltpu
from jax.sharding import PartitionSpec as P

BETA_ONE = 0.9
BETA_TWO = 0.95
RATE = 0.1
DECAY = 0.1
ADAM_EPS = 1e-08
PEAK_EPS = 1e-06
CLIP_RMS = 0.5

NY, NZ, NX, NC = 4, 16, 4, 2
NT, SLOTS, R, COLS = 128, 4, 4, 768
CB = COLS // 128
BLKS = CB * R
E = BLKS * 128
YE = E // NY
PER = YE // NZ
YB = BLKS // NY
MESH = pl.DeviceIdType.MESH
BF, F32 = jnp.bfloat16, jnp.float32

KINDS = ("sy", "sz", "gy", "gz", "qw", "qz", "dz", "dy", "az", "ay", "mw", "mz")
SEND = {name: i for i, name in enumerate(KINDS)}
RECV, _total = {}, 0
for _name in KINDS:
    RECV[_name] = _total
    _total += {"gy": NZ, "gz": 3, "az": NZ}.get(_name, 1)
NW = NY * NX * NC
DIRECT = (8, 4, -4, 2, -2, 1, -1, 0)
SPREAD = (4, -4, 8, 3, -3, 2, -2, 1, -1)


def far_offset(j):
    return 8 + (1 - 2 * (j & 1)) * ((j + 1) >> 1)


def relayed(i):
    p = i >> 1
    return 1 - 2 * (i & 1), 7 - p - (p + 1 >> 2)


def adam(g, step, master, first, second):
    m = BETA_ONE * first + (1.0 - BETA_ONE) * g
    v = BETA_TWO * second + (1.0 - BETA_TWO) * g * g
    one = 1.0 - jnp.exp(step * jnp.log(jnp.full_like(step, BETA_ONE)))
    two = 1.0 - jnp.exp(step * jnp.log(jnp.full_like(step, BETA_TWO)))
    m_hat = m / one
    v_hat = v / two
    w = master - RATE * (m_hat / (jnp.sqrt(v_hat) + ADAM_EPS) + DECAY * master)
    return w, m, v


def kernel(
    g_ref, gs_ref, own_ref, step_ref, w_ref, m_ref, v_ref,
    agb, nv, peak_ref,
    gv, gsv, ownv, stepv, peakv, fs, tv, sv, sf, ysf, ys, syr, st, szs, szr,
    yr, zs, rr, zr, sbp, dsend, dr, dys, dyr, s2, nvs,
    qws, qwr, qzs, qzr, mws, mwr, mzs, mzr,
    wown, zg,
    lsem, ssem, rsem, ready,
):
    dp, tp = lax.axis_index("dp"), lax.axis_index("tensor")
    y, z = dp >> 4, dp & (NZ - 1)
    w_me = y * (NX * NC) + tp

    def at_z(zz):
        return (y * NZ + zz, tp)

    def at_y(yy):
        return (yy * NZ + z, tp)

    def at_w(k):
        return (((y + (k >> 3)) & (NY - 1)) * NZ + z, (tp + k) & (NX * NC - 1))

    def near(d):
        return (z + d + NZ) & (NZ - 1)

    def send(kind, i, src, dst, dev):
        pltpu.make_async_remote_copy(
            src_ref=src, dst_ref=dst, send_sem=ssem.at[SEND[kind]],
            recv_sem=rsem.at[RECV[kind] + i], device_id=dev, device_id_type=MESH,
        ).start()

    def arrived(kind, i, ref):
        pltpu.make_async_copy(ref, ref, rsem.at[RECV[kind] + i]).wait()

    def sent(kind, ref):
        pltpu.make_async_copy(ref, ref, ssem.at[SEND[kind]]).wait()

    barrier = pltpu.get_barrier_semaphore()

    def greet(device):
        pl.semaphore_signal(barrier, inc=1, device_id=device, device_id_type=MESH)

    for d in (4, -4, 3, -3, 2, -2, 1, -1):
        greet(at_z(near(d)))
    for k in (4, 5, 3, 2, 6, 7, 1):
        greet(at_w(k))
    for k in (2, 1, 3):
        greet(at_y((y + k) & (NY - 1)))

    state = (w_ref, m_ref, v_ref)

    def g_copy(cb):
        return pltpu.make_async_copy(g_ref.at[:, :, pl.ds(cb * 128, 128)], gv.at[cb], lsem.at[cb])

    def s_copy(a, cb):
        return pltpu.make_async_copy(
            state[a].at[:, :, pl.ds(cb * 128, 128)], sv.at[a, cb], lsem.at[CB + a * CB + cb]
        )

    gs_copy = pltpu.make_async_copy(gs_ref, gsv, lsem.at[4 * CB])
    own_copy = pltpu.make_async_copy(own_ref, ownv, lsem.at[4 * CB + 1])
    gs_copy.start()
    for cb in range(CB):
        g_copy(cb).start()
    own_copy.start()
    step_copy = pltpu.make_async_copy(step_ref, stepv, lsem.at[4 * CB + 2])
    step_copy.start()
    for a in range(3):
        for cb in range(CB):
            s_copy(a, cb).start()

    gs_copy.wait()
    scales = gsv[...]
    g2 = gv.reshape(CB, NT * R, 128)
    for cb in range(CB):
        g_copy(cb).wait()
        fs[...] = g2[cb].astype(F32)
        for r in range(R):
            block = fs[pl.ds(r, NT, stride=R), :]
            tv[pl.ds((cb * R + r) * 128, 128), :] = (block.T * scales).astype(BF)

    for a in range(3):
        for cb in range(CB):
            s_copy(a, cb).wait()
    sf[...] = sv.reshape(3 * CB * SLOTS * R, 128)[...].astype(F32)
    ysf[...] = jnp.zeros_like(ysf)
    for a in range(3):
        for r in range(R):
            rows = sf[pl.ds(a * CB * SLOTS * R + r, CB * SLOTS, stride=R), :]
            ysf[:, pl.ds(r * 16 + a * 4, 4), :] = rows.reshape(CB, SLOTS, 128)
    ys[...] = ysf[...].reshape(NY, YB * 16, 128).astype(BF)

    pl.semaphore_wait(barrier, 8 + (NX * NC - 1) + (NY - 1))

    for k in range(1, NY):
        yy = (y + k) & (NY - 1)
        send("sy", 0, ys.at[yy], syr.at[y], at_y(yy))
    syr[y] = ys[y]

    def slice_at(ref, yy, zz):
        return ref.at[pl.ds(pl.multiple_of((yy * NZ + zz) * PER, 16), PER)]

    def y_send(i, zz):
        for k in range(1, NY):
            yy = (y + k) & (NY - 1)
            send("gy", i, slice_at(tv, yy, zz), yr.at[i, k - 1], at_y(yy))

    def y_send_relayed(i, carry):
        side, far = relayed(i)
        y_send(i, near(side * far))
        return carry

    lax.fori_loop(0, 8, y_send_relayed, 0)
    for i, d in enumerate(DIRECT):
        y_send(8 + i, near(d))

    for d in (4, -4):
        pl.semaphore_signal(ready, inc=1, device_id=at_z(near(d)), device_id_type=MESH)

    def y_sum(i, zz):
        total = slice_at(tv, y, zz)[...].astype(F32)
        arrived("gy", i, yr.at[i])
        for k in range(3):
            total = total + yr[i, k].astype(F32)
        return total

    def to_relay(i, carry):
        side, far = relayed(i)
        zs[i] = y_sum(i, near(side * far)).astype(BF)
        send("gz", 1 + (i & 1), zs.at[i], rr.at[i & 1, i >> 1], at_z(near(side * (far - 4))))
        return carry

    lax.fori_loop(0, 8, to_relay, 0)
    pl.semaphore_wait(ready, 2)
    for i, d in enumerate(DIRECT[:-1]):
        total = y_sum(8 + i, near(d))
        if abs(d) == 4:
            side = 0 if d > 0 else 1
            arrived("gz", 1 + side, rr.at[side])
            for k in range(4):
                total = total + rr[side, k].astype(F32)
        zs[8 + i] = total.astype(BF)
        send("gz", 0, zs.at[8 + i], zr.at[i], at_z(near(d)))
    mine = y_sum(NZ - 1, z)

    arrived("sy", 0, syr.at[pl.ds(0, NY - 1)])
    for b in range(YB):
        block = syr[:, pl.ds(b * 16, 16), :].reshape(NY * 16, 128).astype(F32)
        block = jnp.concatenate([block, jnp.zeros((128 - NY * 16, 128), F32)], axis=0)
        st[pl.ds(b * 128, 128), :] = block.T
    for zz in range(NZ):
        upper = st[pl.ds(zz * PER, 16), :] + pltpu.roll(st[pl.ds(zz * PER + 16, 16), :], 64, 1)
        szs[zz, pl.ds(0, 16), :] = upper.astype(BF)
        szs[zz, pl.ds(16, 16), :] = st[pl.ds(zz * PER + 32, 16), :].astype(BF)

    own_copy.wait()
    step_copy.wait()
    own = ownv[...]
    spread = jnp.broadcast_to(own.astype(F32), (NT, NT))
    same = spread == spread.T
    before = lax.broadcasted_iota(jnp.int32, (NT, NT), 0) < lax.broadcasted_iota(jnp.int32, (NT, NT), 1)
    slot = jnp.sum(jnp.where(same & before, 1.0, 0.0), axis=0, keepdims=True).astype(jnp.int32)
    own_z, own_y = own & (NZ - 1), own >> 4
    count = jnp.sum(jnp.where(own == dp, 1.0, 0.0), axis=1, keepdims=True)
    place = own_z * 16 + own_y * 4 + slot
    hot = jnp.where(
        lax.broadcasted_iota(jnp.int32, (NZ * 16, NT), 0) == place, 1.0, 0.0
    ).astype(BF)

    arrived("gz", 0, zr)
    summed = mine
    for i in range(len(DIRECT) - 1):
        summed = summed + zr[i].astype(F32)

    def w_stage(kind, value, sendbuf, buf):
        sendbuf[...] = value
        buf[w_me] = value

        def body(i, carry):
            send(kind, 0, sendbuf, buf.at[w_me], at_w(NW - 1 - i))
            return carry

        lax.fori_loop(0, NW - 1, body, 0)

    def w_wait(kind, buf):
        arrived(kind, 0, buf.at[pl.ds(0, NW - 1)])

    def z_stage(kind, value, sendbuf, buf):
        sendbuf[...] = value
        buf[z] = value

        def body(j, carry):
            send(kind, 0, sendbuf, buf.at[z], at_z(near(far_offset(j))))
            return carry

        lax.fori_loop(0, NZ - 1, body, 0)

    def z_wait(kind, buf):
        arrived(kind, 0, buf.at[pl.ds(0, NZ - 1)])

    squares = jnp.sum((summed * summed).reshape(PER // 8, 8, 128), axis=0)
    w_stage("qw", squares, qws, qwr)

    def sz_send(j, carry):
        zz = near(far_offset(j))
        send("sz", 0, szs.at[zz], szr.at[z], at_z(zz))
        return carry

    lax.fori_loop(0, NZ - 1, sz_send, 0)
    szr[z] = szs[z]

    sum_bf = summed.astype(BF)
    sbp[...] = jnp.zeros_like(sbp)
    sbp[pl.ds(0, PER), :] = sum_bf
    dsend[...] = (
        lax.dot_general(hot, sbp[...], (((1,), (1,)), ((), ())), preferred_element_type=F32)
        .astype(BF)
        .reshape(NZ, 16, 128)
    )
    sent("sy", syr.at[pl.ds(0, NY - 1)])
    sent("gy", yr)
    sent("gz", zs)

    w_wait("qw", qwr)
    z_stage("qz", jnp.sum(qwr[...], axis=0), qzs, qzr)

    def d_send(j, carry):
        zz = near(far_offset(j))
        send("dz", 0, dsend.at[zz], dr.at[z], at_z(zz))
        return carry

    lax.fori_loop(0, NZ - 1, d_send, 0)
    dr[z] = dsend[z]

    z_wait("sz", szr)
    low = lax.broadcasted_iota(jnp.int32, (16, 128), 1) < 64
    parts = [[], [], []]
    for pair in range(NZ // 2):
        even0, even1 = szr[2 * pair, pl.ds(0, 16), :].astype(F32), szr[2 * pair, pl.ds(16, 16), :].astype(F32)
        odd0, odd1 = szr[2 * pair + 1, pl.ds(0, 16), :].astype(F32), szr[2 * pair + 1, pl.ds(16, 16), :].astype(F32)
        parts[0].append(jnp.where(low, even0, pltpu.roll(odd0, 64, 1)))
        parts[1].append(jnp.where(low, pltpu.roll(even0, 64, 1), odd0))
        parts[2].append(jnp.where(low, even1, pltpu.roll(odd1, 64, 1)))
    packed = jnp.concatenate([jnp.concatenate(p, axis=1) for p in parts], axis=0).astype(BF)
    target = own_z * 64 + own_y * 16 + slot
    rows = lax.broadcasted_iota(jnp.int32, (NZ * 64, NT), 0)
    old = []
    for a in range(3):
        pick = jnp.where(rows == target + 4 * a, 1.0, 0.0).astype(BF)
        old.append(jnp.dot(packed, pick, preferred_element_type=F32))
    sent("qw", qwr.at[pl.ds(0, NW - 1)])
    sent("sz", szs.at[pl.ds(0, NZ - 1)])

    z_wait("qz", qzr)
    all_squares = jnp.sum(jnp.sum(qzr[...], axis=0), axis=(0, 1), keepdims=True)
    entries = float(NT * R * COLS * NX * NC)
    factor = jnp.minimum(
        1.0, CLIP_RMS * jnp.sqrt(jnp.full((1, 1), entries, F32)) / jnp.sqrt(all_squares + 1e-06)
    )
    step = jnp.full((1, 1), stepv[0].astype(F32), F32)

    new_w, _, _ = adam(sum_bf.astype(F32) * factor, step, old[0], old[1], old[2])
    new_w = new_w.astype(BF)
    wown[...] = new_w
    zg[z] = new_w

    for d in SPREAD:
        send("az", d % NZ, wown, zg.at[z], at_z(near(d)))
    for k in (2, 1, 3):
        send("ay", 0, wown, slice_at(agb, y, z), at_y((y + k) & (NY - 1)))
    peak = jnp.max(jnp.abs(new_w.astype(F32)).reshape(PER // 8, 8, 128), axis=0)
    w_stage("mw", peak, mws, mwr)

    def take(d):
        arrived("az", d % NZ, zg.at[near(-d)])

    def pass_z(d):
        side = 1 if d > 0 else -1
        for s in (3, 2, 1):
            send("az", (d + side * s) % NZ, zg.at[near(-d)], zg.at[near(-d)], at_z(near(side * s)))

    def pass_y(d):
        zz = near(-d)
        for k in (2, 1, 3):
            send("ay", 0, zg.at[zz], slice_at(agb, y, zz), at_y((y + k) & (NY - 1)))

    for d in (1, -1, 2, -2):
        take(d)
        pass_y(d)
    for d in (4, -4):
        take(d)
        pass_z(d)
    for d in (3, -3):
        take(d)
        pass_y(d)
    for d in (4, -4):
        pass_y(d)

    z_wait("dz", dr)
    lane = lax.broadcasted_iota(jnp.int32, (16, 128), 1)
    for b in range(YB):
        block = jnp.zeros((16, 128), F32)
        for zz in range(NZ):
            start = zz * PER - b * 128
            if -PER < start < 128:
                piece = dr[zz].astype(F32)
                if start % 128:
                    piece = pltpu.roll(piece, start % 128, 1)
                if start < 0:
                    piece = jnp.where(lane < start + PER, piece, 0.0)
                elif start + PER > 128:
                    piece = jnp.where(lane >= start, piece, 0.0)
                block = block + piece
        dys[:, pl.ds(b * 4, 4), :] = block.reshape(NY, SLOTS, 128)
    for k in (2, 1, 3):
        yy = (y + k) & (NY - 1)
        send("dy", 0, dys.at[yy], dyr.at[y], at_y(yy))
    dyr[y] = dys[y]

    w_wait("mw", mwr)
    z_stage("mz", jnp.max(mwr[...], axis=0), mzs, mzr)
    for d in (5, -5, 8, 6, -6, 7, -7):
        take(d)
        pass_y(d)
    keep_group = pltpu.make_async_copy(
        zg.reshape(YE, NT), agb.at[pl.ds(pl.multiple_of(y * YE, 16), YE)], lsem.at[4 * CB + 2]
    )
    keep_group.start()
    sent("qz", qzr.at[pl.ds(0, NZ - 1)])
    sent("dz", dsend.at[pl.ds(0, NZ - 1)])
    sent("az", zg.at[pl.ds(0, NZ - 1)])
    sent("mw", mwr.at[pl.ds(0, NW - 1)])

    arrived("dy", 0, dyr.at[pl.ds(0, NY - 1)])
    flat = dyr.reshape(NY * YB * SLOTS, 128)
    for s in range(SLOTS):
        rows_s = flat[pl.ds(s, BLKS, stride=SLOTS), :]
        s2[:, pl.ds(s * R, R), :] = rows_s.reshape(CB, R, 128)
    sums = s2[...].reshape(CB * SLOTS * R, 128)
    size = CB * SLOTS * R
    olds = [sf[pl.ds(a * size, size), :] for a in range(3)]
    news = adam(sums * factor, step, *olds)
    slot_row = (lax.broadcasted_iota(jnp.int32, (size, 128), 0) // R) % SLOTS
    live = slot_row.astype(F32) < count
    nvs2 = nvs.reshape(3, size, 128)
    for a in range(3):
        nvs2[a] = jnp.where(live, news[a], olds[a]).astype(BF)
    keep_new = pltpu.make_async_copy(nvs, nv, lsem.at[4 * CB])
    keep_new.start()

    z_wait("mz", mzr)
    peakv[...] = jnp.max(jnp.max(mzr[...], axis=0), axis=0, keepdims=True) + PEAK_EPS
    keep_peak = pltpu.make_async_copy(peakv, peak_ref, lsem.at[4 * CB + 1])
    keep_peak.start()
    sent("dy", dys.at[pl.ds(0, NY - 1)])
    sent("mz", mzr.at[pl.ds(0, NZ - 1)])
    keep_new.wait()
    keep_peak.wait()
    keep_group.wait()
    arrived("ay", 0, agb.at[pl.ds(0, (NY - 1) * NZ * PER)])
    sent("ay", agb.at[pl.ds(0, (NY - 1) * NZ * PER)])


def finish(agb, nv, peak_ref, nw_ref, nm_ref, nv_ref, quant_ref, scale_ref, peakv, nvv, tv, fs, ov, sem):
    outs = (nw_ref, nm_ref, nv_ref)

    def o_copy(a, cb):
        return pltpu.make_async_copy(
            nvv.at[a, cb], outs[a].at[:, :, pl.ds(cb * 128, 128)], sem.at[CB + a * CB + cb]
        )

    def t_copy(cb):
        rows = pl.ds(cb * R * 128, R * 128)
        return pltpu.make_async_copy(agb.at[rows], tv.at[rows], sem.at[cb])

    def q_copy(cb):
        return pltpu.make_async_copy(ov.at[cb], quant_ref.at[:, :, pl.ds(cb * 128, 128)], sem.at[cb])

    peak_copy = pltpu.make_async_copy(peak_ref, peakv, sem.at[4 * CB])
    peak_copy.start()
    nv_copy = pltpu.make_async_copy(nv, nvv, sem.at[4 * CB + 1])
    for cb in range(CB):
        t_copy(cb).start()
    nv_copy.start()
    peak_copy.wait()
    keep_peak = pltpu.make_async_copy(peakv, scale_ref, sem.at[4 * CB])
    keep_peak.start()
    nv_copy.wait()
    for a in range(3):
        for cb in range(CB):
            o_copy(a, cb).start()
    inverse = 1.0 / peakv[...]
    o2 = ov.reshape(CB, NT * R, 128)
    for cb in range(CB):
        t_copy(cb).wait()
        for r in range(R):
            block = tv[pl.ds((cb * R + r) * 128, 128), :].astype(F32) * inverse
            fs[pl.ds(r, NT, stride=R), :] = block.T
        o2[cb] = fs[...].astype(BF)
        q_copy(cb).start()
    for a in range(3):
        for cb in range(CB):
            o_copy(a, cb).wait()
    for cb in range(CB):
        q_copy(cb).wait()
    keep_peak.wait()


def local(grad_values, grad_scales, owner_ids, step_count, master, moment1, moment2):
    hbm = pl.BlockSpec(memory_space=pltpu.HBM)
    owned = jax.ShapeDtypeStruct((SLOTS, R, COLS), BF)
    V = pltpu.VMEM
    one = V((8, 128), F32)
    exchange = [one, V((NW, 8, 128), F32), one, V((NZ, 8, 128), F32)]
    agb, news, peaks = pl.pallas_call(
        kernel,
        out_shape=(
            jax.ShapeDtypeStruct((E, NT), BF),
            jax.ShapeDtypeStruct((3, CB, SLOTS, R, 128), BF),
            jax.ShapeDtypeStruct((1, NT), F32),
        ),
        in_specs=[hbm] * 7,
        out_specs=(hbm, hbm, hbm),
        scratch_shapes=[
            V((CB, NT, R, 128), BF),
            V((1, NT), F32),
            V((1, NT), jnp.int32),
            pltpu.SMEM((1,), jnp.int32),
            V((1, NT), F32),
            V((NT * R, 128), F32),
            V((E, NT), BF),
            V((3, CB, SLOTS, R, 128), BF),
            V((3 * CB * SLOTS * R, 128), F32),
            V((CB, R * 16, 128), F32),
            V((NY, YB * 16, 128), BF),
            V((NY, YB * 16, 128), BF),
            V((YE, 128), F32),
            V((NZ, 32, 128), BF),
            V((NZ, 32, 128), BF),
            V((NZ, 3, PER, NT), BF),
            V((NZ - 1, PER, NT), BF),
            V((2, 4, PER, NT), BF),
            V((len(DIRECT) - 1, PER, NT), BF),
            V((128, NT), BF),
            V((NZ, 16, 128), BF),
            V((NZ, 16, 128), BF),
            V((NY, YB * SLOTS, 128), F32),
            V((NY, YB * SLOTS, 128), F32),
            V((CB, SLOTS * R, 128), F32),
            V((3, CB, SLOTS, R, 128), BF),
        ]
        + exchange
        + exchange
        + [
            V((PER, NT), BF),
            V((NZ, PER, NT), BF),
            pltpu.SemaphoreType.DMA((4 * CB + 3,)),
            pltpu.SemaphoreType.DMA((len(KINDS),)),
            pltpu.SemaphoreType.DMA((_total,)),
            pltpu.SemaphoreType.REGULAR,
        ],
        compiler_params=pltpu.CompilerParams(
            collective_id=0, has_side_effects=True, vmem_limit_bytes=62 << 20
        ),
        name="exchange",
    )(
        grad_values[0], grad_scales, owner_ids.reshape(1, NT), step_count,
        master[0], moment1[0], moment2[0],
    )
    out = pl.pallas_call(
        finish,
        out_shape=(
            owned, owned, owned,
            jax.ShapeDtypeStruct((NT, R, COLS), BF),
            jax.ShapeDtypeStruct((1, NT), F32),
        ),
        in_specs=[hbm, hbm, hbm],
        out_specs=(hbm,) * 5,
        scratch_shapes=[
            V((1, NT), F32),
            V((3, CB, SLOTS, R, 128), BF),
            V((E, NT), BF),
            V((NT * R, 128), F32),
            V((CB, NT, R, 128), BF),
            pltpu.SemaphoreType.DMA((4 * CB + 2,)),
        ],
        compiler_params=pltpu.CompilerParams(vmem_limit_bytes=62 << 20),
        name="finish",
    )(agb, news, peaks)
    return out[0][None], out[1][None], out[2][None], out[3], out[4].reshape(NT)


def solution(mesh):
    split = P("dp", None, None, "tensor")
    return jax.shard_map(
        local,
        mesh=mesh,
        in_specs=(split, P("dp", None), P(), P(), split, split, split),
        out_specs=(split, split, split, P(None, None, "tensor"), P()),
        check_vma=False,
    )
```

time: 91.4 us -> 63.6 us (0.70)
  Pallas kernels: 82.5 us -> 61.7 us
  local copies, waits for them, and re-layouts: 7.21 us -> 0 us
    pallas_call x1 -> x2, Pallas kernels: 82.5 us -> 61.7 us  [the longest x1 58.6 us: local(): pl.pallas_call(kernel, out_shape=(jax.ShapeDtypeStruct((E, NT), BF), jax....]
    unnamed x17 -> x0, local copies, waits for them, and re-layouts: 7.21 us -> none
where the time goes in v2:
time: 63.6 us; the launch traced here: 63 us
  Pallas kernels  61.7 us (97%)
  between operations  1.29 us (2%)
    pallas_call x1, Pallas kernels, local(): pl.pallas_call(kernel, out_shape=(jax.ShapeDtypeStruct((E, NT), BF), jax....  58.6 us
    pallas_call x1, Pallas kernels, local(): pl.pallas_call(finish, out_shape=(owned, owned, owned, jax.ShapeDtypeStru...  3.13 us

profile of v2, /device:TPU:1, one launch (start us, length us, event | category | flops | bytes accessed | tf_op | source)
XLA Modules:
  0.0 63.0 jit_solution(11679962148315138227)
XLA Ops:
  1.3 58.6 %exchange.1 = (bf16[3072,128]{1,0:T(8,128)(2,1)}, bf16[3,6,4,4,128]{4,3,2,1,0:T(4,128)(2,1)}, f32[1,128]{1,0:T(1,128)}) custom-call(bf16[128,4,768]{2,1,0:T(4,128)(2,1)} %bitcast.9, f32[1,128]{1,0:T(1,128)} %gs_ref.1, s32[1,128]{1,0:T(1,128)} %bitcast.13, s32[1]{0:T(128)S(6)} %copy.12.step_ref, bf16[4,4,768]{2,1,0:T(4,128)(2,1)} %bitcast.10, ...), custom_call_target="tpu_custom_call" | custom-call | tf_op jit(solution)/shard_map/exchange/pallas_call | solution.py:472
  59.8 3.1 %finish.1 = (bf16[4,4,768]{2,1,0:T(4,128)(2,1)}, bf16[4,4,768]{2,1,0:T(4,128)(2,1)}, bf16[4,4,768]{2,1,0:T(4,128)(2,1)}, bf16[128,4,768]{2,1,0:T(4,128)(2,1)}, f32[1,128]{1,0:T(1,128)}) custom-call(bf16[3072,128]{1,0:T(8,128)(2,1)} %get-tuple-element.13.agb, bf16[3,6,4,4,128]{4,3,2,1,0:T(4,128)(2,1)} %get-tuple-element.14.nv, ...), custom_call_target="tpu_custom_call" | custom-call | tf_op jit(solution)/shard_map/finish/pallas_call | solution.py:527

commit v3 on v2

--- a/solution.py
+++ b/solution.py
@@ -24,15 +24,19 @@
 MESH = pl.DeviceIdType.MESH
 BF, F32 = jnp.bfloat16, jnp.float32
 
-KINDS = ("sy", "sz", "gy", "gz", "qw", "qz", "dz", "dy", "az", "ay", "mw", "mz")
+KINDS = ("sy", "sz", "gn", "gy", "gz", "qw", "qz", "dz", "dy", "az", "ay", "mw", "mz")
 SEND = {name: i for i, name in enumerate(KINDS)}
 RECV, _total = {}, 0
 for _name in KINDS:
+    if _name == "az":
+        RECV[_name] = RECV["gy"]
+        continue
     RECV[_name] = _total
-    _total += {"gy": NZ, "gz": 3, "az": NZ}.get(_name, 1)
+    _total += {"gy": NZ, "gz": 3}.get(_name, 1)
 NW = NY * NX * NC
-DIRECT = (8, 4, -4, 2, -2, 1, -1, 0)
-SPREAD = (4, -4, 8, 3, -3, 2, -2, 1, -1)
+CLOSE = (2, -2, 1, -1)
+DIRECT = (8, 4, -4, 3, -3, 0)
+SPREAD = (4, -4, 1, -1, 8, 2, -2, 3, -3)
 
 
 def far_offset(j):
@@ -40,8 +44,7 @@
 
 
 def relayed(i):
-    p = i >> 1
-    return 1 - 2 * (i & 1), 7 - p - (p + 1 >> 2)
+    return 1 - 2 * (i & 1), 7 - (i >> 1)
 
 
 def adam(g, step, master, first, second):
@@ -59,7 +62,7 @@
     g_ref, gs_ref, own_ref, step_ref, w_ref, m_ref, v_ref,
     agb, nv, peak_ref,
     gv, gsv, ownv, stepv, peakv, fs, tv, sv, sf, ysf, ys, syr, st, szs, szr,
-    yr, zs, rr, zr, sbp, dsend, dr, dys, dyr, s2, nvs,
+    nb, close, closeb, yr, zs, rr, zr, sbp, dsend, dr, dys, dyr, s2, nvs,
     qws, qwr, qzs, qzr, mws, mwr, mzs, mzr,
     wown, zg,
     lsem, ssem, rsem, ready,
@@ -111,34 +114,32 @@
 
     def s_copy(a, cb):
         return pltpu.make_async_copy(
-            state[a].at[:, :, pl.ds(cb * 128, 128)], sv.at[a, cb], lsem.at[CB + a * CB + cb]
+            state[a].at[:, :, pl.ds(cb * 128, 128)], sv.at[a, cb], lsem.at[CB]
         )
 
-    gs_copy = pltpu.make_async_copy(gs_ref, gsv, lsem.at[4 * CB])
-    own_copy = pltpu.make_async_copy(own_ref, ownv, lsem.at[4 * CB + 1])
+    gs_copy = pltpu.make_async_copy(gs_ref, gsv, lsem.at[CB + 1])
+    own_copy = pltpu.make_async_copy(own_ref, ownv, lsem.at[CB + 2])
     gs_copy.start()
     for cb in range(CB):
         g_copy(cb).start()
     own_copy.start()
-    step_copy = pltpu.make_async_copy(step_ref, stepv, lsem.at[4 * CB + 2])
+    step_copy = pltpu.make_async_copy(step_ref, stepv, lsem.at[CB + 3])
     step_copy.start()
     for a in range(3):
         for cb in range(CB):
             s_copy(a, cb).start()
 
     gs_copy.wait()
-    scales = gsv[...]
+    scales = jnp.broadcast_to(gsv[...], (NT, NT)).T
     g2 = gv.reshape(CB, NT * R, 128)
     for cb in range(CB):
         g_copy(cb).wait()
         fs[...] = g2[cb].astype(F32)
         for r in range(R):
             block = fs[pl.ds(r, NT, stride=R), :]
-            tv[pl.ds((cb * R + r) * 128, 128), :] = (block.T * scales).astype(BF)
-
-    for a in range(3):
-        for cb in range(CB):
-            s_copy(a, cb).wait()
+            tv[pl.ds((cb * R + r) * 128, 128), :] = (block * scales).astype(BF).T
+
+    pltpu.make_async_copy(sv, sv, lsem.at[CB]).wait()
     sf[...] = sv.reshape(3 * CB * SLOTS * R, 128)[...].astype(F32)
     ysf[...] = jnp.zeros_like(ysf)
     for a in range(3):
@@ -154,11 +155,15 @@
         send("sy", 0, ys.at[yy], syr.at[y], at_y(yy))
     syr[y] = ys[y]
 
+    tv4 = tv.reshape(NY, NZ, PER, NT)
+    for i, d in enumerate(CLOSE):
+        send("gn", 0, tv4.at[:, near(d)], nb.at[i], at_z(near(d)))
+
     def slice_at(ref, yy, zz):
         return ref.at[pl.ds(pl.multiple_of((yy * NZ + zz) * PER, 16), PER)]
 
     def y_send(i, zz):
-        for k in range(1, NY):
+        for k in (2, 1, 3):
             yy = (y + k) & (NY - 1)
             send("gy", i, slice_at(tv, yy, zz), yr.at[i, k - 1], at_y(yy))
 
@@ -167,38 +172,54 @@
         y_send(i, near(side * far))
         return carry
 
-    lax.fori_loop(0, 8, y_send_relayed, 0)
-    for i, d in enumerate(DIRECT):
-        y_send(8 + i, near(d))
+    lax.fori_loop(0, 6, y_send_relayed, 0)
+    for i, d in enumerate(DIRECT[:-1]):
+        y_send(6 + i, near(d))
 
     for d in (4, -4):
         pl.semaphore_signal(ready, inc=1, device_id=at_z(near(d)), device_id_type=MESH)
 
-    def y_sum(i, zz):
-        total = slice_at(tv, y, zz)[...].astype(F32)
+    def y_sum(i, total):
         arrived("gy", i, yr.at[i])
         for k in range(3):
             total = total + yr[i, k].astype(F32)
         return total
 
+    def part_of(zz):
+        return slice_at(tv, y, zz)[...].astype(F32)
+
     def to_relay(i, carry):
         side, far = relayed(i)
-        zs[i] = y_sum(i, near(side * far)).astype(BF)
+        zs[i] = y_sum(i, part_of(near(side * far))).astype(BF)
         send("gz", 1 + (i & 1), zs.at[i], rr.at[i & 1, i >> 1], at_z(near(side * (far - 4))))
         return carry
 
-    lax.fori_loop(0, 8, to_relay, 0)
+    lax.fori_loop(0, 2, to_relay, 0)
+
+    arrived("gn", 0, nb)
+    for yy in range(NY):
+        total = tv4[yy, z].astype(F32)
+        for i in range(len(CLOSE)):
+            total = total + nb[i, yy].astype(F32)
+        close[yy] = total
+        closeb[yy] = total.astype(BF)
+    last = 6 + len(DIRECT) - 1
+    for k in (2, 1, 3):
+        yy = (y + k) & (NY - 1)
+        send("gy", last, closeb.at[yy], yr.at[last, k - 1], at_y(yy))
+
+    lax.fori_loop(2, 6, to_relay, 0)
     pl.semaphore_wait(ready, 2)
     for i, d in enumerate(DIRECT[:-1]):
-        total = y_sum(8 + i, near(d))
+        total = y_sum(6 + i, part_of(near(d)))
         if abs(d) == 4:
             side = 0 if d > 0 else 1
             arrived("gz", 1 + side, rr.at[side])
-            for k in range(4):
+            for k in range(3):
                 total = total + rr[side, k].astype(F32)
-        zs[8 + i] = total.astype(BF)
-        send("gz", 0, zs.at[8 + i], zr.at[i], at_z(near(d)))
-    mine = y_sum(NZ - 1, z)
+        zs[6 + i] = total.astype(BF)
+        send("gz", 0, zs.at[6 + i], zr.at[i], at_z(near(d)))
+    mine = y_sum(last, close[y])
 
     arrived("sy", 0, syr.at[pl.ds(0, NY - 1)])
     for b in range(YB):
@@ -255,7 +276,7 @@
     def z_wait(kind, buf):
         arrived(kind, 0, buf.at[pl.ds(0, NZ - 1)])
 
-    squares = jnp.sum((summed * summed).reshape(PER // 8, 8, 128), axis=0)
+    squares = jnp.sum(summed * summed, axis=0, keepdims=True)
     w_stage("qw", squares, qws, qwr)
 
     def sz_send(j, carry):
@@ -275,6 +296,7 @@
         .reshape(NZ, 16, 128)
     )
     sent("sy", syr.at[pl.ds(0, NY - 1)])
+    sent("gn", nb)
     sent("gy", yr)
     sent("gz", zs)
 
@@ -314,7 +336,7 @@
     factor = jnp.minimum(
         1.0, CLIP_RMS * jnp.sqrt(jnp.full((1, 1), entries, F32)) / jnp.sqrt(all_squares + 1e-06)
     )
-    step = jnp.full((1, 1), stepv[0].astype(F32), F32)
+    step = stepv[...].astype(F32)
 
     new_w, _, _ = adam(sum_bf.astype(F32) * factor, step, old[0], old[1], old[2])
     new_w = new_w.astype(BF)
@@ -323,10 +345,10 @@
 
     for d in SPREAD:
         send("az", d % NZ, wown, zg.at[z], at_z(near(d)))
+    peak = jnp.max(jnp.abs(new_w.astype(F32)), axis=0, keepdims=True)
+    w_stage("mw", peak, mws, mwr)
     for k in (2, 1, 3):
         send("ay", 0, wown, slice_at(agb, y, z), at_y((y + k) & (NY - 1)))
-    peak = jnp.max(jnp.abs(new_w.astype(F32)).reshape(PER // 8, 8, 128), axis=0)
-    w_stage("mw", peak, mws, mwr)
 
     def take(d):
         arrived("az", d % NZ, zg.at[near(-d)])
@@ -380,7 +402,7 @@
         take(d)
         pass_y(d)
     keep_group = pltpu.make_async_copy(
-        zg.reshape(YE, NT), agb.at[pl.ds(pl.multiple_of(y * YE, 16), YE)], lsem.at[4 * CB + 2]
+        zg.reshape(YE, NT), agb.at[pl.ds(pl.multiple_of(y * YE, 16), YE)], lsem.at[CB + 3]
     )
     keep_group.start()
     sent("qz", qzr.at[pl.ds(0, NZ - 1)])
@@ -399,15 +421,16 @@
     news = adam(sums * factor, step, *olds)
     slot_row = (lax.broadcasted_iota(jnp.int32, (size, 128), 0) // R) % SLOTS
     live = slot_row.astype(F32) < count
-    nvs2 = nvs.reshape(3, size, 128)
     for a in range(3):
-        nvs2[a] = jnp.where(live, news[a], olds[a]).astype(BF)
-    keep_new = pltpu.make_async_copy(nvs, nv, lsem.at[4 * CB])
+        kept = jnp.where(live, news[a], olds[a]).reshape(CB, SLOTS, R, 128).astype(BF)
+        for cb in range(CB):
+            nvs[a, :, :, pl.ds(cb * 128, 128)] = kept[cb]
+    keep_new = pltpu.make_async_copy(nvs, nv, lsem.at[CB + 1])
     keep_new.start()
 
     z_wait("mz", mzr)
-    peakv[...] = jnp.max(jnp.max(mzr[...], axis=0), axis=0, keepdims=True) + PEAK_EPS
-    keep_peak = pltpu.make_async_copy(peakv, peak_ref, lsem.at[4 * CB + 1])
+    peakv[...] = jnp.max(mzr[...], axis=0) + PEAK_EPS
+    keep_peak = pltpu.make_async_copy(peakv, peak_ref, lsem.at[CB + 2])
     keep_peak.start()
     sent("dy", dys.at[pl.ds(0, NY - 1)])
     sent("mz", mzr.at[pl.ds(0, NZ - 1)])
@@ -418,62 +441,61 @@
     sent("ay", agb.at[pl.ds(0, (NY - 1) * NZ * PER)])
 
 
-def finish(agb, nv, peak_ref, nw_ref, nm_ref, nv_ref, quant_ref, scale_ref, peakv, nvv, tv, fs, ov, sem):
+def finish(
+    agb, nv, peak_ref, nw_ref, nm_ref, nv_ref, quant_ref, scale_ref, peakv, nvv, tv, fs, ov, sem
+):
     outs = (nw_ref, nm_ref, nv_ref)
 
-    def o_copy(a, cb):
-        return pltpu.make_async_copy(
-            nvv.at[a, cb], outs[a].at[:, :, pl.ds(cb * 128, 128)], sem.at[CB + a * CB + cb]
-        )
+    def o_copy(a):
+        return pltpu.make_async_copy(nvv.at[a], outs[a], sem.at[CB])
 
     def t_copy(cb):
         rows = pl.ds(cb * R * 128, R * 128)
         return pltpu.make_async_copy(agb.at[rows], tv.at[rows], sem.at[cb])
 
     def q_copy(cb):
-        return pltpu.make_async_copy(ov.at[cb], quant_ref.at[:, :, pl.ds(cb * 128, 128)], sem.at[cb])
-
-    peak_copy = pltpu.make_async_copy(peak_ref, peakv, sem.at[4 * CB])
+        return pltpu.make_async_copy(
+            ov.at[cb], quant_ref.at[:, :, pl.ds(cb * 128, 128)], sem.at[CB + 1]
+        )
+
+    peak_copy = pltpu.make_async_copy(peak_ref, peakv, sem.at[CB + 2])
     peak_copy.start()
-    nv_copy = pltpu.make_async_copy(nv, nvv, sem.at[4 * CB + 1])
     for cb in range(CB):
         t_copy(cb).start()
+    nv_copy = pltpu.make_async_copy(nv, nvv, sem.at[CB])
     nv_copy.start()
     peak_copy.wait()
-    keep_peak = pltpu.make_async_copy(peakv, scale_ref, sem.at[4 * CB])
+    keep_peak = pltpu.make_async_copy(peakv, scale_ref, sem.at[CB + 2])
     keep_peak.start()
-    nv_copy.wait()
-    for a in range(3):
-        for cb in range(CB):
-            o_copy(a, cb).start()
-    inverse = 1.0 / peakv[...]
+    inverse = jnp.broadcast_to(1.0 / peakv[...], (NT, NT)).T
     o2 = ov.reshape(CB, NT * R, 128)
     for cb in range(CB):
         t_copy(cb).wait()
         for r in range(R):
-            block = tv[pl.ds((cb * R + r) * 128, 128), :].astype(F32) * inverse
-            fs[pl.ds(r, NT, stride=R), :] = block.T
+            block = tv[pl.ds((cb * R + r) * 128, 128), :].T
+            fs[pl.ds(r, NT, stride=R), :] = block.astype(F32) * inverse
         o2[cb] = fs[...].astype(BF)
         q_copy(cb).start()
-    for a in range(3):
-        for cb in range(CB):
-            o_copy(a, cb).wait()
-    for cb in range(CB):
-        q_copy(cb).wait()
+        if cb == 0:
+            nv_copy.wait()
+            for a in range(3):
+                o_copy(a).start()
     keep_peak.wait()
+    pltpu.make_async_copy(nvv, nvv, sem.at[CB]).wait()
+    pltpu.make_async_copy(ov, ov, sem.at[CB + 1]).wait()
 
 
 def local(grad_values, grad_scales, owner_ids, step_count, master, moment1, moment2):
     hbm = pl.BlockSpec(memory_space=pltpu.HBM)
     owned = jax.ShapeDtypeStruct((SLOTS, R, COLS), BF)
     V = pltpu.VMEM
-    one = V((8, 128), F32)
-    exchange = [one, V((NW, 8, 128), F32), one, V((NZ, 8, 128), F32)]
+    one = V((1, 128), F32)
+    exchange = [one, V((NW, 1, 128), F32), one, V((NZ, 1, 128), F32)]
     agb, news, peaks = pl.pallas_call(
         kernel,
         out_shape=(
             jax.ShapeDtypeStruct((E, NT), BF),
-            jax.ShapeDtypeStruct((3, CB, SLOTS, R, 128), BF),
+            jax.ShapeDtypeStruct((3, SLOTS, R, COLS), BF),
             jax.ShapeDtypeStruct((1, NT), F32),
         ),
         in_specs=[hbm] * 7,
@@ -482,7 +504,7 @@
             V((CB, NT, R, 128), BF),
             V((1, NT), F32),
             V((1, NT), jnp.int32),
-            pltpu.SMEM((1,), jnp.int32),
+            V((1, 1), jnp.int32),
             V((1, NT), F32),
             V((NT * R, 128), F32),
             V((E, NT), BF),
@@ -494,9 +516,12 @@
             V((YE, 128), F32),
             V((NZ, 32, 128), BF),
             V((NZ, 32, 128), BF),
-            V((NZ, 3, PER, NT), BF),
-            V((NZ - 1, PER, NT), BF),
-            V((2, 4, PER, NT), BF),
+            V((len(CLOSE), NY, PER, NT), BF),
+            V((NY, PER, NT), F32),
+            V((NY, PER, NT), BF),
+            V((6 + len(DIRECT), 3, PER, NT), BF),
+            V((5 + len(DIRECT), PER, NT), BF),
+            V((2, 3, PER, NT), BF),
             V((len(DIRECT) - 1, PER, NT), BF),
             V((128, NT), BF),
             V((NZ, 16, 128), BF),
@@ -504,14 +529,14 @@
             V((NY, YB * SLOTS, 128), F32),
             V((NY, YB * SLOTS, 128), F32),
             V((CB, SLOTS * R, 128), F32),
-            V((3, CB, SLOTS, R, 128), BF),
+            V((3, SLOTS, R, COLS), BF),
         ]
         + exchange
         + exchange
         + [
             V((PER, NT), BF),
             V((NZ, PER, NT), BF),
-            pltpu.SemaphoreType.DMA((4 * CB + 3,)),
+            pltpu.SemaphoreType.DMA((CB + 4,)),
             pltpu.SemaphoreType.DMA((len(KINDS),)),
             pltpu.SemaphoreType.DMA((_total,)),
             pltpu.SemaphoreType.REGULAR,
@@ -521,7 +546,7 @@
         ),
         name="exchange",
     )(
-        grad_values[0], grad_scales, owner_ids.reshape(1, NT), step_count,
+        grad_values[0], grad_scales, owner_ids.reshape(1, NT), step_count.reshape(1, 1),
         master[0], moment1[0], moment2[0],
     )
     out = pl.pallas_call(
@@ -535,11 +560,11 @@
         out_specs=(hbm,) * 5,
         scratch_shapes=[
             V((1, NT), F32),
-            V((3, CB, SLOTS, R, 128), BF),
+            V((3, SLOTS, R, COLS), BF),
             V((E, NT), BF),
             V((NT * R, 128), F32),
             V((CB, NT, R, 128), BF),
-            pltpu.SemaphoreType.DMA((4 * CB + 2,)),
+            pltpu.SemaphoreType.DMA((CB + 3,)),
         ],
         compiler_params=pltpu.CompilerParams(vmem_limit_bytes=62 << 20),
         name="finish",

time: 63.6 us -> 60.6 us (0.953)
  Pallas kernels: 61.7 us -> 58.5 us
    pallas_call x1, Pallas kernels: 58.6 us -> 55.9 us  [local(): pl.pallas_call(kernel, out_shape=(jax.ShapeDtypeStruct((E, NT), BF), jax....]
where the time goes in v3:
time: 60.6 us; the launch traced here: 59.8 us
  Pallas kernels  58.5 us (97%)
  between operations  1.29 us (2%)
    pallas_call x1, Pallas kernels, local(): pl.pallas_call(kernel, out_shape=(jax.ShapeDtypeStruct((E, NT), BF), jax....  55.9 us
    pallas_call x1, Pallas kernels, local(): pl.pallas_call(finish, out_shape=(owned, owned, owned, jax.ShapeDtypeStru...  2.6 us

profile of v3, /device:TPU:1, one launch (start us, length us, event | category | flops | bytes accessed | tf_op | source)
XLA Modules:
  0.0 59.8 jit_solution(7663897358992388847)
XLA Ops:
  1.3 55.9 %exchange.1 = (bf16[3072,128]{1,0:T(8,128)(2,1)}, bf16[3,4,4,768]{3,2,1,0:T(4,128)(2,1)}, f32[1,128]{1,0:T(1,128)}) custom-call(bf16[128,4,768]{2,1,0:T(4,128)(2,1)} %bitcast.11, f32[1,128]{1,0:T(1,128)} %gs_ref.1, s32[1,128]{1,0:T(1,128)} %bitcast.15, s32[1,1]{1,0:T(1,128)} %bitcast.10.step_ref, bf16[4,4,768]{2,1,0:T(4,128)(2,1)} %bitcast.12, ...), custom_call_target="tpu_custom_call" | custom-call | tf_op jit(solution)/shard_map/exchange/pallas_call | solution.py:494
  57.2 2.6 %finish.1 = (bf16[4,4,768]{2,1,0:T(4,128)(2,1)}, bf16[4,4,768]{2,1,0:T(4,128)(2,1)}, bf16[4,4,768]{2,1,0:T(4,128)(2,1)}, bf16[128,4,768]{2,1,0:T(4,128)(2,1)}, f32[1,128]{1,0:T(1,128)}) custom-call(bf16[3072,128]{1,0:T(8,128)(2,1)} %get-tuple-element.13.agb, bf16[3,4,4,768]{3,2,1,0:T(4,128)(2,1)} %get-tuple-element.14.nv, f32[1,128]{1,0:T(1,128)} %get-tuple-element.15.peak_ref), custom_call_target="tpu_custom_call" | custom-call | tf_op jit(solution)/shard_map/finish/pallas_call | solution.py:552

commit v4 on v3

--- a/solution.py
+++ b/solution.py
@@ -24,7 +24,7 @@
 MESH = pl.DeviceIdType.MESH
 BF, F32 = jnp.bfloat16, jnp.float32
 
-KINDS = ("sy", "sz", "gn", "gy", "gz", "qw", "qz", "dz", "dy", "az", "ay", "mw", "mz")
+KINDS = ("sy", "sz", "gn", "gy", "gz", "qw", "qz", "dz", "dy", "az", "ay", "an", "ac", "mw", "mz")
 SEND = {name: i for i, name in enumerate(KINDS)}
 RECV, _total = {}, 0
 for _name in KINDS:
@@ -35,8 +35,9 @@
     _total += {"gy": NZ, "gz": 3}.get(_name, 1)
 NW = NY * NX * NC
 CLOSE = (2, -2, 1, -1)
-DIRECT = (8, 4, -4, 3, -3, 0)
-SPREAD = (4, -4, 1, -1, 8, 2, -2, 3, -3)
+DIRECT = (8, 3, -3, 4, -4, 0)
+WITH_Y = (1, -1)
+SPREAD = (4, -4, 8, 2, -2, 3, -3)
 
 
 def far_offset(j):
@@ -64,8 +65,8 @@
     gv, gsv, ownv, stepv, peakv, fs, tv, sv, sf, ysf, ys, syr, st, szs, szr,
     nb, close, closeb, yr, zs, rr, zr, sbp, dsend, dr, dys, dyr, s2, nvs,
     qws, qwr, qzs, qzr, mws, mwr, mzs, mzr,
-    wown, zg,
-    lsem, ssem, rsem, ready,
+    wown, zg, zn,
+    lsem, ssem, rsem, ready, ready_far,
 ):
     dp, tp = lax.axis_index("dp"), lax.axis_index("tensor")
     y, z = dp >> 4, dp & (NZ - 1)
@@ -100,7 +101,7 @@
     def greet(device):
         pl.semaphore_signal(barrier, inc=1, device_id=device, device_id_type=MESH)
 
-    for d in (4, -4, 3, -3, 2, -2, 1, -1):
+    for d in (2, -2, 1, -1):
         greet(at_z(near(d)))
     for k in (4, 5, 3, 2, 6, 7, 1):
         greet(at_w(k))
@@ -148,7 +149,7 @@
             ysf[:, pl.ds(r * 16 + a * 4, 4), :] = rows.reshape(CB, SLOTS, 128)
     ys[...] = ysf[...].reshape(NY, YB * 16, 128).astype(BF)
 
-    pl.semaphore_wait(barrier, 8 + (NX * NC - 1) + (NY - 1))
+    pl.semaphore_wait(barrier, 4 + (NX * NC - 1) + (NY - 1))
 
     for k in range(1, NY):
         yy = (y + k) & (NY - 1)
@@ -163,7 +164,7 @@
         return ref.at[pl.ds(pl.multiple_of((yy * NZ + zz) * PER, 16), PER)]
 
     def y_send(i, zz):
-        for k in (2, 1, 3):
+        for k in (1, 3, 2):
             yy = (y + k) & (NY - 1)
             send("gy", i, slice_at(tv, yy, zz), yr.at[i, k - 1], at_y(yy))
 
@@ -176,8 +177,11 @@
     for i, d in enumerate(DIRECT[:-1]):
         y_send(6 + i, near(d))
 
-    for d in (4, -4):
-        pl.semaphore_signal(ready, inc=1, device_id=at_z(near(d)), device_id_type=MESH)
+    def tell(sem, hops):
+        for d in (hops, -hops):
+            pl.semaphore_signal(sem, inc=1, device_id=at_z(near(d)), device_id_type=MESH)
+
+    tell(ready, 2)
 
     def y_sum(i, total):
         arrived("gy", i, yr.at[i])
@@ -194,6 +198,8 @@
         send("gz", 1 + (i & 1), zs.at[i], rr.at[i & 1, i >> 1], at_z(near(side * (far - 4))))
         return carry
 
+    pl.semaphore_wait(ready, 2)
+    tell(ready_far, 4)
     lax.fori_loop(0, 2, to_relay, 0)
 
     arrived("gn", 0, nb)
@@ -209,7 +215,7 @@
         send("gy", last, closeb.at[yy], yr.at[last, k - 1], at_y(yy))
 
     lax.fori_loop(2, 6, to_relay, 0)
-    pl.semaphore_wait(ready, 2)
+    pl.semaphore_wait(ready_far, 2)
     for i, d in enumerate(DIRECT[:-1]):
         total = y_sum(6 + i, part_of(near(d)))
         if abs(d) == 4:
@@ -341,17 +347,19 @@
     new_w, _, _ = adam(sum_bf.astype(F32) * factor, step, old[0], old[1], old[2])
     new_w = new_w.astype(BF)
     wown[...] = new_w
-    zg[z] = new_w
+    zn[y] = new_w
 
     for d in SPREAD:
         send("az", d % NZ, wown, zg.at[z], at_z(near(d)))
     peak = jnp.max(jnp.abs(new_w.astype(F32)), axis=0, keepdims=True)
     w_stage("mw", peak, mws, mwr)
     for k in (2, 1, 3):
-        send("ay", 0, wown, slice_at(agb, y, z), at_y((y + k) & (NY - 1)))
+        send("an", 0, wown, zn.at[y], at_y((y + k) & (NY - 1)))
 
     def take(d):
-        arrived("az", d % NZ, zg.at[near(-d)])
+        zz = near(-d)
+        arrived("az", d % NZ, zg.at[zz])
+        pltpu.make_async_copy(zg.at[zz], agb.at[y, zz], lsem.at[CB + 3]).start()
 
     def pass_z(d):
         side = 1 if d > 0 else -1
@@ -361,9 +369,14 @@
     def pass_y(d):
         zz = near(-d)
         for k in (2, 1, 3):
-            send("ay", 0, zg.at[zz], slice_at(agb, y, zz), at_y((y + k) & (NY - 1)))
-
-    for d in (1, -1, 2, -2):
+            send("ay", 0, zg.at[zz], agb.at[y, zz], at_y((y + k) & (NY - 1)))
+
+    arrived("an", 0, zn.at[pl.ds(0, NY - 1)])
+    for d in WITH_Y:
+        send("ac", 0, zn, agb.at[:, z], at_z(near(d)))
+    keep_own = pltpu.make_async_copy(zn, agb.at[:, z], lsem.at[CB + 1])
+    keep_own.start()
+    for d in (2, -2):
         take(d)
         pass_y(d)
     for d in (4, -4):
@@ -401,13 +414,13 @@
     for d in (5, -5, 8, 6, -6, 7, -7):
         take(d)
         pass_y(d)
-    keep_group = pltpu.make_async_copy(
-        zg.reshape(YE, NT), agb.at[pl.ds(pl.multiple_of(y * YE, 16), YE)], lsem.at[CB + 3]
-    )
-    keep_group.start()
     sent("qz", qzr.at[pl.ds(0, NZ - 1)])
     sent("dz", dsend.at[pl.ds(0, NZ - 1)])
-    sent("az", zg.at[pl.ds(0, NZ - 1)])
+    keep_own.wait()
+    sent("an", zg.at[pl.ds(0, NY - 1)])
+    sent("ac", tv.at[pl.ds(0, len(WITH_Y) * NY * PER)])
+    slices = NZ - 1 - len(WITH_Y)
+    sent("az", zg.at[pl.ds(0, slices)])
     sent("mw", mwr.at[pl.ds(0, NW - 1)])
 
     arrived("dy", 0, dyr.at[pl.ds(0, NY - 1)])
@@ -436,9 +449,10 @@
     sent("mz", mzr.at[pl.ds(0, NZ - 1)])
     keep_new.wait()
     keep_peak.wait()
-    keep_group.wait()
-    arrived("ay", 0, agb.at[pl.ds(0, (NY - 1) * NZ * PER)])
-    sent("ay", agb.at[pl.ds(0, (NY - 1) * NZ * PER)])
+    pltpu.make_async_copy(zg.at[pl.ds(0, slices)], zg.at[pl.ds(0, slices)], lsem.at[CB + 3]).wait()
+    arrived("ac", 0, tv.at[pl.ds(0, len(WITH_Y) * NY * PER)])
+    arrived("ay", 0, tv.at[pl.ds(0, (NY - 1) * slices * PER)])
+    sent("ay", tv.at[pl.ds(0, (NY - 1) * slices * PER)])
 
 
 def finish(
@@ -494,7 +508,7 @@
     agb, news, peaks = pl.pallas_call(
         kernel,
         out_shape=(
-            jax.ShapeDtypeStruct((E, NT), BF),
+            jax.ShapeDtypeStruct((NY, NZ, PER, NT), BF),
             jax.ShapeDtypeStruct((3, SLOTS, R, COLS), BF),
             jax.ShapeDtypeStruct((1, NT), F32),
         ),
@@ -536,9 +550,11 @@
         + [
             V((PER, NT), BF),
             V((NZ, PER, NT), BF),
+            V((NY, PER, NT), BF),
             pltpu.SemaphoreType.DMA((CB + 4,)),
             pltpu.SemaphoreType.DMA((len(KINDS),)),
             pltpu.SemaphoreType.DMA((_total,)),
+            pltpu.SemaphoreType.REGULAR,
             pltpu.SemaphoreType.REGULAR,
         ],
         compiler_params=pltpu.CompilerParams(
@@ -568,7 +584,7 @@
         ],
         compiler_params=pltpu.CompilerParams(vmem_limit_bytes=62 << 20),
         name="finish",
-    )(agb, news, peaks)
+    )(agb.reshape(E, NT), news, peaks)
     return out[0][None], out[1][None], out[2][None], out[3], out[4].reshape(NT)
 
 

time: 60.6 us -> 58.7 us (0.969)
  Pallas kernels: 58.5 us -> 56.9 us
    pallas_call x1, Pallas kernels: 55.9 us -> 54.3 us  [local(): pl.pallas_call(kernel, out_shape=(jax.ShapeDtypeStruct((NY, NZ, PER, NT),...]
where the time goes in v4:
time: 58.7 us; the launch traced here: 58.2 us
  Pallas kernels  56.9 us (97%)
  between operations  1.29 us (2%)
    pallas_call x1, Pallas kernels, local(): pl.pallas_call(kernel, out_shape=(jax.ShapeDtypeStruct((NY, NZ, PER, NT),...  54.3 us
    pallas_call x1, Pallas kernels, local(): pl.pallas_call(finish, out_shape=(owned, owned, owned, jax.ShapeDtypeStru...  2.6 us

profile of v4, /device:TPU:1, one launch (start us, length us, event | category | flops | bytes accessed | tf_op | source)
XLA Modules:
  0.0 58.2 jit_solution(7768763230920305624)
XLA Ops:
  1.3 54.3 %exchange.1 = (bf16[4,16,48,128]{3,2,1,0:T(8,128)(2,1)}, bf16[3,4,4,768]{3,2,1,0:T(4,128)(2,1)}, f32[1,128]{1,0:T(1,128)}) custom-call(bf16[128,4,768]{2,1,0:T(4,128)(2,1)} %bitcast.12, f32[1,128]{1,0:T(1,128)} %gs_ref.1, s32[1,128]{1,0:T(1,128)} %bitcast.17, s32[1,1]{1,0:T(1,128)} %bitcast.11.step_ref, bf16[4,4,768]{2,1,0:T(4,128)(2,1)} %bitcast.14, ...), custom_call_target="tpu_custom_call" | custom-call | tf_op jit(solution)/shard_map/exchange/pallas_call | solution.py:508
  55.6 2.6 %finish.1 = (bf16[4,4,768]{2,1,0:T(4,128)(2,1)}, bf16[4,4,768]{2,1,0:T(4,128)(2,1)}, bf16[4,4,768]{2,1,0:T(4,128)(2,1)}, bf16[128,4,768]{2,1,0:T(4,128)(2,1)}, f32[1,128]{1,0:T(1,128)}) custom-call(bf16[3072,128]{1,0:T(8,128)(2,1)} %bitcast.13, bf16[3,4,4,768]{3,2,1,0:T(4,128)(2,1)} %get-tuple-element.14.nv, f32[1,128]{1,0:T(1,128)} %get-tuple-element.15.peak_ref), custom_call_target="tpu_custom_call" | custom-call | tf_op jit(solution)/shard_map/finish/pallas_call | solution.py:568

commit v5 on v4

--- a/solution.py
+++ b/solution.py
@@ -151,31 +151,31 @@
 
     pl.semaphore_wait(barrier, 4 + (NX * NC - 1) + (NY - 1))
 
+    tv4 = tv.reshape(NY, NZ, PER, NT)
+    for i, d in enumerate(CLOSE):
+        send("gn", 0, tv4.at[:, near(d)], nb.at[i], at_z(near(d)))
+
+    def slice_at(ref, yy, zz):
+        return ref.at[pl.ds(pl.multiple_of((yy * NZ + zz) * PER, 16), PER)]
+
+    def y_send(i, zz):
+        for k in (1, 3, 2):
+            yy = (y + k) & (NY - 1)
+            send("gy", i, slice_at(tv, yy, zz), yr.at[i, k - 1], at_y(yy))
+
+    def y_send_relayed(i, carry):
+        side, far = relayed(i)
+        y_send(i, near(side * far))
+        return carry
+
+    lax.fori_loop(0, 6, y_send_relayed, 0)
+    for i, d in enumerate(DIRECT[:-1]):
+        y_send(6 + i, near(d))
+
     for k in range(1, NY):
         yy = (y + k) & (NY - 1)
         send("sy", 0, ys.at[yy], syr.at[y], at_y(yy))
     syr[y] = ys[y]
-
-    tv4 = tv.reshape(NY, NZ, PER, NT)
-    for i, d in enumerate(CLOSE):
-        send("gn", 0, tv4.at[:, near(d)], nb.at[i], at_z(near(d)))
-
-    def slice_at(ref, yy, zz):
-        return ref.at[pl.ds(pl.multiple_of((yy * NZ + zz) * PER, 16), PER)]
-
-    def y_send(i, zz):
-        for k in (1, 3, 2):
-            yy = (y + k) & (NY - 1)
-            send("gy", i, slice_at(tv, yy, zz), yr.at[i, k - 1], at_y(yy))
-
-    def y_send_relayed(i, carry):
-        side, far = relayed(i)
-        y_send(i, near(side * far))
-        return carry
-
-    lax.fori_loop(0, 6, y_send_relayed, 0)
-    for i, d in enumerate(DIRECT[:-1]):
-        y_send(6 + i, near(d))
 
     def tell(sem, hops):
         for d in (hops, -hops):
@@ -200,7 +200,7 @@
 
     pl.semaphore_wait(ready, 2)
     tell(ready_far, 4)
-    lax.fori_loop(0, 2, to_relay, 0)
+    lax.fori_loop(0, 4, to_relay, 0)
 
     arrived("gn", 0, nb)
     for yy in range(NY):
@@ -210,11 +210,11 @@
         close[yy] = total
         closeb[yy] = total.astype(BF)
     last = 6 + len(DIRECT) - 1
-    for k in (2, 1, 3):
+    for k in (1, 3, 2):
         yy = (y + k) & (NY - 1)
         send("gy", last, closeb.at[yy], yr.at[last, k - 1], at_y(yy))
 
-    lax.fori_loop(2, 6, to_relay, 0)
+    lax.fori_loop(4, 6, to_relay, 0)
     pl.semaphore_wait(ready_far, 2)
     for i, d in enumerate(DIRECT[:-1]):
         total = y_sum(6 + i, part_of(near(d)))

time: 58.7 us -> 57.7 us (0.983)
  Pallas kernels: 56.9 us -> 56.2 us
    pallas_call x1, Pallas kernels: 54.3 us -> 53.6 us  [local(): pl.pallas_call(kernel, out_shape=(jax.ShapeDtypeStruct((NY, NZ, PER, NT),...]
where the time goes in v5:
time: 57.7 us; the launch traced here: 57.5 us
  Pallas kernels  56.2 us (97%)
  between operations  1.29 us (2%)
    pallas_call x1, Pallas kernels, local(): pl.pallas_call(kernel, out_shape=(jax.ShapeDtypeStruct((NY, NZ, PER, NT),...  53.6 us
    pallas_call x1, Pallas kernels, local(): pl.pallas_call(finish, out_shape=(owned, owned, owned, jax.ShapeDtypeStru...  2.6 us

profile of v5, /device:TPU:1, one launch (start us, length us, event | category | flops | bytes accessed | tf_op | source)
XLA Modules:
  0.0 57.5 jit_solution(9110181483050492927)
XLA Ops:
  1.3 53.6 %exchange.1 = (bf16[4,16,48,128]{3,2,1,0:T(8,128)(2,1)}, bf16[3,4,4,768]{3,2,1,0:T(4,128)(2,1)}, f32[1,128]{1,0:T(1,128)}) custom-call(bf16[128,4,768]{2,1,0:T(4,128)(2,1)} %bitcast.12, f32[1,128]{1,0:T(1,128)} %gs_ref.1, s32[1,128]{1,0:T(1,128)} %bitcast.17, s32[1,1]{1,0:T(1,128)} %bitcast.11.step_ref, bf16[4,4,768]{2,1,0:T(4,128)(2,1)} %bitcast.14, ...), custom_call_target="tpu_custom_call" | custom-call | tf_op jit(solution)/shard_map/exchange/pallas_call | solution.py:508
  54.9 2.6 %finish.1 = (bf16[4,4,768]{2,1,0:T(4,128)(2,1)}, bf16[4,4,768]{2,1,0:T(4,128)(2,1)}, bf16[4,4,768]{2,1,0:T(4,128)(2,1)}, bf16[128,4,768]{2,1,0:T(4,128)(2,1)}, f32[1,128]{1,0:T(1,128)}) custom-call(bf16[3072,128]{1,0:T(8,128)(2,1)} %bitcast.13, bf16[3,4,4,768]{3,2,1,0:T(4,128)(2,1)} %get-tuple-element.14.nv, f32[1,128]{1,0:T(1,128)} %get-tuple-element.15.peak_ref), custom_call_target="tpu_custom_call" | custom-call | tf_op jit(solution)/shard_map/finish/pallas_call | solution.py:568

commit v6 on v5

--- a/solution.py
+++ b/solution.py
@@ -200,7 +200,7 @@
 
     pl.semaphore_wait(ready, 2)
     tell(ready_far, 4)
-    lax.fori_loop(0, 4, to_relay, 0)
+    lax.fori_loop(0, 6, to_relay, 0)
 
     arrived("gn", 0, nb)
     for yy in range(NY):
@@ -214,7 +214,6 @@
         yy = (y + k) & (NY - 1)
         send("gy", last, closeb.at[yy], yr.at[last, k - 1], at_y(yy))
 
-    lax.fori_loop(4, 6, to_relay, 0)
     pl.semaphore_wait(ready_far, 2)
     for i, d in enumerate(DIRECT[:-1]):
         total = y_sum(6 + i, part_of(near(d)))

time: 57.7 us -> 57.7 us (level)
  no operation moved by 1% of the time
where the time goes in v6:
time: 57.7 us; the launch traced here: 57.4 us
  Pallas kernels  56.1 us (97%)
  between operations  1.29 us (2%)
    pallas_call x1, Pallas kernels, local(): pl.pallas_call(kernel, out_shape=(jax.ShapeDtypeStruct((NY, NZ, PER, NT),...  53.5 us
    pallas_call x1, Pallas kernels, local(): pl.pallas_call(finish, out_shape=(owned, owned, owned, jax.ShapeDtypeStru...  2.6 us

profile of v6, /device:TPU:1, one launch (start us, length us, event | category | flops | bytes accessed | tf_op | source)
XLA Modules:
  0.0 57.4 jit_solution(7563687874471807105)
XLA Ops:
  1.3 53.5 %exchange.1 = (bf16[4,16,48,128]{3,2,1,0:T(8,128)(2,1)}, bf16[3,4,4,768]{3,2,1,0:T(4,128)(2,1)}, f32[1,128]{1,0:T(1,128)}) custom-call(bf16[128,4,768]{2,1,0:T(4,128)(2,1)} %bitcast.12, f32[1,128]{1,0:T(1,128)} %gs_ref.1, s32[1,128]{1,0:T(1,128)} %bitcast.17, s32[1,1]{1,0:T(1,128)} %bitcast.11.step_ref, bf16[4,4,768]{2,1,0:T(4,128)(2,1)} %bitcast.14, ...), custom_call_target="tpu_custom_call" | custom-call | tf_op jit(solution)/shard_map/exchange/pallas_call | solution.py:507
  54.8 2.6 %finish.1 = (bf16[4,4,768]{2,1,0:T(4,128)(2,1)}, bf16[4,4,768]{2,1,0:T(4,128)(2,1)}, bf16[4,4,768]{2,1,0:T(4,128)(2,1)}, bf16[128,4,768]{2,1,0:T(4,128)(2,1)}, f32[1,128]{1,0:T(1,128)}) custom-call(bf16[3072,128]{1,0:T(8,128)(2,1)} %bitcast.13, bf16[3,4,4,768]{3,2,1,0:T(4,128)(2,1)} %get-tuple-element.14.nv, f32[1,128]{1,0:T(1,128)} %get-tuple-element.15.peak_ref), custom_call_target="tpu_custom_call" | custom-call | tf_op jit(solution)/shard_map/finish/pallas_call | solution.py:567
